TPU v7x, 256 devices: a whole 4x4x8 slice. The times are simulated.
256 devices in a mesh: seq: 16 (over z, core), chan: 16 (over y, x).
Axes of the slice: x: 4, y: 4, z: 8, core: 2. Of those that a mesh axis runs over, the one named last changes fastest.
Arguments:
- tokens: bfloat16 [4096, 4096], P('seq', 'chan'), may hold values from -6 to 6
- in_weight: bfloat16 [4096, 3, 4096], P(None, None, 'chan'), may hold values from -0.09375 to 0.09375
- short_taps: float32 [3, 3, 4096], P(None, None, 'chan'), may hold values from -3.5 to 3.5
- filter_in: float32 [33, 64], replicated, may hold values from -1.5 to 1.5
- filter_out: float32 [64, 4096], P(None, 'chan'), may hold values from -0.75 to 0.75
- rates: float32 [4096], P('chan'), may hold values from 1.2207031e-05 to 0.034
- skip: float32 [4096], P('chan'), may hold values from -1 to 1
- out_weight: bfloat16 [4096, 4096], P('chan'), may hold values from -0.09375 to 0.09375
Outputs:
- mixed: bfloat16 [4096, 4096], P('seq', 'chan')
All inputs are finite; a program needn't handle non-finite values.
Results may differ from a plain program's by a relative error of at most 0.02.
Values may be sent and summed in bfloat16 or wider, within the bound.
A program may use at most 128 MiB of HBM per device.

v0:
```python
import math

import jax
import jax.numpy as jnp
from jax import lax
from jax.sharding import PartitionSpec as P


def shifted(value, axis, by):
    count = lax.axis_size(axis)
    pairs = [(i, i + by) for i in range(count) if 0 <= i + by < count]
    return lax.ppermute(value, axis, pairs)


def filter_values(positions, seq_total, filter_in, filter_out, rates):
    freq_count = (filter_in.shape[0] - 1) // 2
    freqs = 1 + jnp.arange(freq_count, dtype=jnp.int32) * (seq_total // 4 - 1) // (freq_count - 1)
    phase = positions[:, None] * freqs[None, :] % seq_total
    angle = phase.astype(jnp.float32) * (2.0 * math.pi / seq_total)
    places = positions.astype(jnp.float32)
    feats = jnp.concatenate([places[:, None] / seq_total, jnp.cos(angle), jnp.sin(angle)], axis=1)
    inner = jnp.sin(jnp.dot(feats, filter_in, precision=lax.Precision.HIGHEST))
    shaped = jnp.dot(inner, filter_out, precision=lax.Precision.HIGHEST)
    return shaped * jnp.sqrt(rates)[None, :] * jnp.exp(-rates[None, :] * places[:, None])


def tables(block_rows):
    length = 2 * block_rows
    freq_index = jnp.arange(length, dtype=jnp.int32)
    time_index = jnp.arange(block_rows, dtype=jnp.int32)
    factor = 2.0 * math.pi / length
    ang_fwd = (freq_index[:, None] * time_index[None, :] % length).astype(jnp.float32) * factor
    forward = jnp.concatenate([jnp.cos(ang_fwd), -jnp.sin(ang_fwd)], axis=0)
    ang_inv = (freq_index[None, :] * (time_index[:, None] + block_rows) % length).astype(
        jnp.float32
    ) * factor
    inverse = jnp.concatenate([jnp.cos(ang_inv), -jnp.sin(ang_inv)], axis=1) / length
    parity = 1.0 - 2.0 * (freq_index % 2).astype(jnp.float32)
    signs = jnp.concatenate([parity, parity], axis=0)
    return (forward, inverse, signs)


def complex_product(left, right, half):
    left_re, left_im = (left[..., :half, :], left[..., half:, :])
    right_re, right_im = (right[..., :half, :], right[..., half:, :])
    return jnp.concatenate(
        [left_re * right_re - left_im * right_im, left_re * right_im + left_im * right_re], axis=-2
    )


def lag_spectra(segments, forward, signs):
    spectra = jnp.einsum("kb,nbc->nkc", forward, segments, precision=lax.Precision.HIGHEST)
    earlier = jnp.concatenate([jnp.zeros_like(spectra[:1]), spectra[:-1]], axis=0)
    return earlier + signs[None, :, None] * spectra


def per_device(tokens, in_weight, short_taps, filter_in, filter_out, rates, skip, out_weight):
    local_rows = tokens.shape[0]
    local_chans = rates.shape[0]
    model_width = in_weight.shape[0]
    seq_count = lax.axis_size("seq")
    seq_total = local_rows * seq_count
    half = 2 * local_rows
    flat_weight = in_weight.reshape(model_width, 3 * local_chans)
    projected = jnp.dot(
        lax.all_gather(tokens, "chan", axis=1, tiled=True),
        flat_weight,
        preferred_element_type=jnp.float32,
    )
    projected = projected.astype(jnp.bfloat16).reshape(local_rows, 3, local_chans)
    prior = shifted(projected[local_rows - 2 :], "seq", 1)
    padded = jnp.concatenate([prior, projected], axis=0).astype(jnp.float32)
    branch = jnp.zeros((local_rows, 3, local_chans), jnp.float32)
    for lag in range(3):
        branch = branch + short_taps[lag][None] * padded[2 - lag : 2 - lag + local_rows]
    query = branch[:, 0]
    drive = (branch[:, 1] * branch[:, 2]).astype(jnp.bfloat16)
    drive_f = drive.astype(jnp.float32)
    forward, inverse, signs = tables(local_rows)
    own_positions = lax.axis_index("seq") * local_rows + jnp.arange(local_rows, dtype=jnp.int32)
    own_filter = filter_values(own_positions, seq_total, filter_in, filter_out, rates)
    whole_filter = lax.all_gather(
        own_filter.astype(jnp.bfloat16), "seq", axis=0, tiled=True
    ).astype(own_filter.dtype)
    lags = lag_spectra(whole_filter.reshape(seq_count, local_rows, local_chans), forward, signs)

    def absorb(total_spec, block, step):
        block_spec = jnp.dot(forward, block.astype(jnp.float32), precision=lax.Precision.HIGHEST)
        lag_spec = lax.dynamic_index_in_dim(lags, step, 0, keepdims=False)
        return total_spec + complex_product(lag_spec, block_spec, half)

    def advance(step, carried):
        block, total_spec = carried
        total_spec = absorb(total_spec, block, step)
        return (shifted(block, "seq", 1), total_spec)

    start_spec = jnp.zeros((2 * half, local_chans), jnp.float32)
    block, total_spec = lax.fori_loop(0, seq_count - 1, advance, (drive, start_spec))
    total_spec = absorb(total_spec, block, seq_count - 1)
    conv = jnp.dot(inverse, total_spec, precision=lax.Precision.HIGHEST)
    conv = conv + skip[None, :] * drive_f
    gated = (query * conv).astype(jnp.bfloat16)
    summed = lax.psum_scatter(
        lax.dot_general(
            out_weight, gated, (((0,), (1,)), ((), ())), preferred_element_type=jnp.float32
        ).astype(jnp.bfloat16),
        "chan",
        scatter_dimension=0,
        tiled=True,
    ).astype(jnp.float32)
    return summed.T.astype(jnp.bfloat16)


def solution(mesh):
    placed = (
        P("seq", "chan"),
        P(None, None, "chan"),
        P(None, None, "chan"),
        P(),
        P(None, "chan"),
        P("chan"),
        P("chan"),
        P("chan", None),
    )
    return jax.shard_map(
        per_device, mesh=mesh, in_specs=placed, out_specs=P("seq", "chan"), check_vma=False
    )
```

profile of v0, /device:TPU:1, one launch (start us, length us, event | category | flops | bytes accessed | tf_op | source)
XLA Modules:
  0.0 379.8 jit_solution(16308281864606939341)
XLA Ops:
  11.5 8.7 %copy.25 = bf16[4096,3,256]{0,2,1:T(8,128)(2,1)} copy(bf16[4096,3,256]{2,0,1:T(8,128)(2,1)} %param.11) | data formatting | bytes 12582912 | tf_op args[1]
  23.6 3.3 fusion.29
  26.8 28.0 %all-gather.5.cloned.1.call-done = bf16[4096,256]{1,0:T(8,128)(2,1)} async-done(((bf16[256,256]{1,0:T(8,128)(2,1)}), bf16[4096,256]{1,0:T(8,128)(2,1)}) %all-gather.5.cloned.1.call-update) | async-done | bytes 2097168 | tf_op jit(solution)/shard_map/all_gather | solution.py:82
  54.9 14.1 %convolution_bitcast_fusion = f32[16,1024,256]{1,2,0:T(8,128)} fusion(bf16[16,256,256]{2,1,0:T(8,128)(2,1)} %bitcast.70, f32[512,256]{1,0:T(8,128)S(1)} %get-tuple-element.162, f32[512,256]{1,0:T(8,128)S(1)} %get-tuple-element.163), kind=kOutput, calls=%fused_computation.10 | convolution fusion | flops 12885164032 | bytes 19922944 | tf_op jit(solution)/shard_map/kb,nbc->nkc/dot_general | solution.py:52
  68.9 14.5 %slice.124 = f32[15,1024,256]{1,2,0:T(8,128)} slice(f32[16,1024,256]{1,2,0:T(8,128)} %convolution_bitcast_fusion), slice={[0:15], [0:1024], [0:256]} | slice | bytes 31457280 | tf_op jit(solution)/shard_map/slice | solution.py:53
  83.5 23.5 %all-gather.3.cloned.1.call-done = bf16[256,4096]{1,0:T(8,128)(2,1)} async-done(((bf16[256,256]{1,0:T(8,128)(2,1)}), bf16[256,4096]{1,0:T(8,128)(2,1)}) %all-gather.3.cloned.1.call-update) | async-done | bytes 2097168 | tf_op jit(solution)/shard_map/all_gather | solution.py:66
  107.0 5.3 %convolution_convert_fusion.1 = bf16[256,768]{1,0:T(8,128)(2,1)S(1)} fusion(bf16[256,4096]{1,0:T(8,128)(2,1)} %all-gather.3.cloned.1.call-done, bf16[4096,768]{0,1:T(8,128)(2,1)} %bitcast.69), kind=kOutput, calls=%fused_computation.13 | convolution fusion | flops 1610809344 | bytes 8781824 | tf_op jit(solution)/shard_map/dot_general | solution.py:65
  112.2 4.8 %collective-permute-start.1 = (bf16[2,3,256]{2,0,1:T(2,128)(2,1)S(1)}, bf16[2,3,256]{2,0,1:T(2,128)(2,1)S(1)}, u32[]{:S(2)}, u32[]{:S(2)}) collective-permute-start(bf16[2,3,256]{2,0,1:T(2,128)(2,1)S(1)} %bitcast.72), channel_id=1, source_target_pairs={{0,16},{16,32},{32,48},{48,64},{64,80},{80,96},{96,112},{112,128},... | collective-permute-start | bytes 9224 | tf_op jit(solution)/shard_map/ppermute | solution.py:12
  117.0 17.7 %multiply_add_fusion = f32[16,1024,256]{1,2,0:T(8,128)} fusion(f32[16,1024,256]{1,2,0:T(8,128)} %convolution_bitcast_fusion, f32[15,1024,256]{1,2,0:T(8,128)} %slice.124, f32[1024]{0:T(1024)S(1)} %pad_maximum_fusion.1), kind=kLoop, calls=%fused_computation.9 | loop fusion | flops 8388608 | bytes 49287168 | tf_op jit(solution)/shard_map/add | solution.py:54
  136.4 154.2 %while.16 = (s32[]{:T(128)}, bf16[256,256]{1,0:T(8,128)(2,1)S(1)}, f32[1024,256]{1,0:T(8,128)}, f32[16,1024,256]{1,2,0:T(8,128)}, f32[1024,256]{1,0:T(8,128)}, /*index=5*/s32[]{:T(128)}, s32[]{:T(128)}, s32[]{}) while((s32[]{:T(128)}, bf16[256,256]{1,0:T(8,128)(2,1)S(1)}, f32[1024,256]{1,0:T(8,128)}, f32[16,1024,256]{1,2,0:T(8,128)}, ...), condition=%wide.region_1.2_spmd.clone, body=%wide.region_0.1_spmd.clone.sunk | while | flops 806879232 | bytes 13500571 | solution.py:98
  145.0 3.6 collective-permute-start
  154.1 2.3 maximum_add_fusion.4
  163.9 2.3 maximum_add_fusion.4
  166.3 3.6 collective-permute-start
  175.4 2.3 maximum_add_fusion.4
  185.2 2.3 maximum_add_fusion.4
  187.5 4.8 %collective-permute-start = (bf16[256,256]{1,0:T(8,128)(2,1)S(1)}, bf16[256,256]{1,0:T(8,128)(2,1)S(1)}, u32[]{:S(2)}, u32[]{:S(2)}) collective-permute-start(bf16[256,256]{1,0:T(8,128)(2,1)S(1)} %copy.47), channel_id=1, source_target_pairs={{0,16},{16,32},{32,48},{48,64},{64,80},{80,96},{96,112},{112,128},... | collective-permute-start | bytes 393224 | tf_op jit(solution)/shard_map/while/body/eval_jaxpr/ppermute | solution.py:12
  197.8 2.3 maximum_add_fusion.4
  207.6 2.3 maximum_add_fusion.4
  210.0 2.7 collective-permute-start
  218.2 2.3 maximum_add_fusion.4
  228.0 2.3 maximum_add_fusion.4
  230.4 2.7 collective-permute-start
  238.6 2.3 maximum_add_fusion.4
  248.4 2.3 maximum_add_fusion.4
  250.7 2.7 collective-permute-start
  258.9 2.3 maximum_add_fusion.4
  268.7 2.3 maximum_add_fusion.4
  278.5 2.3 maximum_add_fusion.4
  292.6 2.5 multiply_subtract_fusion
  296.6 2.6 fusion.5
  301.4 72.0 %reduce-scatter.2.cloned.1.call-done = bf16[256,256]{0,1:T(8,128)(2,1)} async-done(((bf16[4096,256]{0,1:T(8,128)(2,1)}), bf16[256,256]{0,1:T(8,128)(2,1)}) %reduce-scatter.2.cloned.1.call-update) | async-done | bytes 131088 | tf_op jit(solution)/shard_map/reduce_scatter | solution.py:103
  (159 shorter events, 118.5 us)
Async XLA Ops:
  6.5 292.7 %copy-start = (bf16[256,4096]{1,0:T(8,128)(2,1)S(1)}, bf16[256,4096]{1,0:T(8,128)(2,1)}, u32[]{:S(2)}) copy-start(bf16[256,4096]{1,0:T(8,128)(2,1)} %param.17) | copy-start | bytes 6291460
  6.5 48.3 %all-gather.5.cloned.1.call-start = ((), (), s32[]{:S(2)}) async-start(), calls=%async_computation.2 | async-start | bytes 2228224 | tf_op jit(solution)/shard_map/all_gather | solution.py:82
  10.7 96.3 %all-gather.3.cloned.1.call-start = ((), (), s32[]{:S(2)}) async-start(), calls=%async_computation.1 | async-start | bytes 2228224 | tf_op jit(solution)/shard_map/all_gather | solution.py:66
  11.5 361.8 %reduce-scatter.2.cloned.1.call-start = ((), (), s32[]{:S(2)}) async-start(), calls=%async_computation.3 | async-start | bytes 2228224 | tf_op jit(solution)/shard_map/reduce_scatter | solution.py:103
  11.5 12.0 %copy-start.4 = (f32[3,3,256]{2,1,0:T(4,128)S(1)}, f32[3,3,256]{2,1,0:T(4,128)}, u32[]{:S(2)}) copy-start(f32[3,3,256]{2,1,0:T(4,128)} %param.12) | copy-start | bytes 27652
  22.3 46.6 %copy-start.1 = (f32[512,256]{1,0:T(8,128)}, f32[512,256]{1,0:T(8,128)S(1)}, u32[]{:S(2)}) copy-start(f32[512,256]{1,0:T(8,128)S(1)} %get-tuple-element.162) | copy-start | bytes 1572868
  22.3 46.6 %copy-start.2 = (f32[512,256]{1,0:T(8,128)}, f32[512,256]{1,0:T(8,128)S(1)}, u32[]{:S(2)}) copy-start(f32[512,256]{1,0:T(8,128)S(1)} %get-tuple-element.163) | copy-start | bytes 1572868
  112.2 22.9 %collective-permute-start.1 = (bf16[2,3,256]{2,0,1:T(2,128)(2,1)S(1)}, bf16[2,3,256]{2,0,1:T(2,128)(2,1)S(1)}, u32[]{:S(2)}, u32[]{:S(2)}) collective-permute-start(bf16[2,3,256]{2,0,1:T(2,128)(2,1)S(1)} %bitcast.72), channel_id=1, source_target_pairs={{0,16},{16,32},{32,48},{48,64},{64,80},{80,96},{96,112},{112,128},... | collective-permute-start | bytes 9224 | tf_op jit(solution)/shard_map/ppermute | solution.py:12
  135.5 0.9 copy-start.3
  136.4 8.6 %collective-permute-start = (bf16[256,256]{1,0:T(8,128)(2,1)S(1)}, bf16[256,256]{1,0:T(8,128)(2,1)S(1)}, u32[]{:S(2)}, u32[]{:S(2)}) collective-permute-start(bf16[256,256]{1,0:T(8,128)(2,1)S(1)} %copy.47), channel_id=1, source_target_pairs={{0,16},{16,32},{32,48},{48,64},{64,80},{80,96},{96,112},{112,128},... | collective-permute-start | bytes 393224 | tf_op jit(solution)/shard_map/while/body/eval_jaxpr/ppermute | solution.py:12
  145.0 11.4 %collective-permute-start = (bf16[256,256]{1,0:T(8,128)(2,1)S(1)}, bf16[256,256]{1,0:T(8,128)(2,1)S(1)}, u32[]{:S(2)}, u32[]{:S(2)}) collective-permute-start(bf16[256,256]{1,0:T(8,128)(2,1)S(1)} %copy.47), channel_id=1, source_target_pairs={{0,16},{16,32},{32,48},{48,64},{64,80},{80,96},{96,112},{112,128},... | collective-permute-start | bytes 393224 | tf_op jit(solution)/shard_map/while/body/eval_jaxpr/ppermute | solution.py:12
  156.5 9.8 %collective-permute-start = (bf16[256,256]{1,0:T(8,128)(2,1)S(1)}, bf16[256,256]{1,0:T(8,128)(2,1)S(1)}, u32[]{:S(2)}, u32[]{:S(2)}) collective-permute-start(bf16[256,256]{1,0:T(8,128)(2,1)S(1)} %copy.47), channel_id=1, source_target_pairs={{0,16},{16,32},{32,48},{48,64},{64,80},{80,96},{96,112},{112,128},... | collective-permute-start | bytes 393224 | tf_op jit(solution)/shard_map/while/body/eval_jaxpr/ppermute | solution.py:12
  166.3 11.4 %collective-permute-start = (bf16[256,256]{1,0:T(8,128)(2,1)S(1)}, bf16[256,256]{1,0:T(8,128)(2,1)S(1)}, u32[]{:S(2)}, u32[]{:S(2)}) collective-permute-start(bf16[256,256]{1,0:T(8,128)(2,1)S(1)} %copy.47), channel_id=1, source_target_pairs={{0,16},{16,32},{32,48},{48,64},{64,80},{80,96},{96,112},{112,128},... | collective-permute-start | bytes 393224 | tf_op jit(solution)/shard_map/while/body/eval_jaxpr/ppermute | solution.py:12
  177.7 9.8 %collective-permute-start = (bf16[256,256]{1,0:T(8,128)(2,1)S(1)}, bf16[256,256]{1,0:T(8,128)(2,1)S(1)}, u32[]{:S(2)}, u32[]{:S(2)}) collective-permute-start(bf16[256,256]{1,0:T(8,128)(2,1)S(1)} %copy.47), channel_id=1, source_target_pairs={{0,16},{16,32},{32,48},{48,64},{64,80},{80,96},{96,112},{112,128},... | collective-permute-start | bytes 393224 | tf_op jit(solution)/shard_map/while/body/eval_jaxpr/ppermute | solution.py:12
  187.5 12.6 %collective-permute-start = (bf16[256,256]{1,0:T(8,128)(2,1)S(1)}, bf16[256,256]{1,0:T(8,128)(2,1)S(1)}, u32[]{:S(2)}, u32[]{:S(2)}) collective-permute-start(bf16[256,256]{1,0:T(8,128)(2,1)S(1)} %copy.47), channel_id=1, source_target_pairs={{0,16},{16,32},{32,48},{48,64},{64,80},{80,96},{96,112},{112,128},... | collective-permute-start | bytes 393224 | tf_op jit(solution)/shard_map/while/body/eval_jaxpr/ppermute | solution.py:12
  200.2 9.8 %collective-permute-start = (bf16[256,256]{1,0:T(8,128)(2,1)S(1)}, bf16[256,256]{1,0:T(8,128)(2,1)S(1)}, u32[]{:S(2)}, u32[]{:S(2)}) collective-permute-start(bf16[256,256]{1,0:T(8,128)(2,1)S(1)} %copy.47), channel_id=1, source_target_pairs={{0,16},{16,32},{32,48},{48,64},{64,80},{80,96},{96,112},{112,128},... | collective-permute-start | bytes 393224 | tf_op jit(solution)/shard_map/while/body/eval_jaxpr/ppermute | solution.py:12
  210.0 10.5 %collective-permute-start = (bf16[256,256]{1,0:T(8,128)(2,1)S(1)}, bf16[256,256]{1,0:T(8,128)(2,1)S(1)}, u32[]{:S(2)}, u32[]{:S(2)}) collective-permute-start(bf16[256,256]{1,0:T(8,128)(2,1)S(1)} %copy.47), channel_id=1, source_target_pairs={{0,16},{16,32},{32,48},{48,64},{64,80},{80,96},{96,112},{112,128},... | collective-permute-start | bytes 393224 | tf_op jit(solution)/shard_map/while/body/eval_jaxpr/ppermute | solution.py:12
  220.6 9.8 %collective-permute-start = (bf16[256,256]{1,0:T(8,128)(2,1)S(1)}, bf16[256,256]{1,0:T(8,128)(2,1)S(1)}, u32[]{:S(2)}, u32[]{:S(2)}) collective-permute-start(bf16[256,256]{1,0:T(8,128)(2,1)S(1)} %copy.47), channel_id=1, source_target_pairs={{0,16},{16,32},{32,48},{48,64},{64,80},{80,96},{96,112},{112,128},... | collective-permute-start | bytes 393224 | tf_op jit(solution)/shard_map/while/body/eval_jaxpr/ppermute | solution.py:12
  230.4 10.5 %collective-permute-start = (bf16[256,256]{1,0:T(8,128)(2,1)S(1)}, bf16[256,256]{1,0:T(8,128)(2,1)S(1)}, u32[]{:S(2)}, u32[]{:S(2)}) collective-permute-start(bf16[256,256]{1,0:T(8,128)(2,1)S(1)} %copy.47), channel_id=1, source_target_pairs={{0,16},{16,32},{32,48},{48,64},{64,80},{80,96},{96,112},{112,128},... | collective-permute-start | bytes 393224 | tf_op jit(solution)/shard_map/while/body/eval_jaxpr/ppermute | solution.py:12
  240.9 9.8 %collective-permute-start = (bf16[256,256]{1,0:T(8,128)(2,1)S(1)}, bf16[256,256]{1,0:T(8,128)(2,1)S(1)}, u32[]{:S(2)}, u32[]{:S(2)}) collective-permute-start(bf16[256,256]{1,0:T(8,128)(2,1)S(1)} %copy.47), channel_id=1, source_target_pairs={{0,16},{16,32},{32,48},{48,64},{64,80},{80,96},{96,112},{112,128},... | collective-permute-start | bytes 393224 | tf_op jit(solution)/shard_map/while/body/eval_jaxpr/ppermute | solution.py:12
  250.7 10.5 %collective-permute-start = (bf16[256,256]{1,0:T(8,128)(2,1)S(1)}, bf16[256,256]{1,0:T(8,128)(2,1)S(1)}, u32[]{:S(2)}, u32[]{:S(2)}) collective-permute-start(bf16[256,256]{1,0:T(8,128)(2,1)S(1)} %copy.47), channel_id=1, source_target_pairs={{0,16},{16,32},{32,48},{48,64},{64,80},{80,96},{96,112},{112,128},... | collective-permute-start | bytes 393224 | tf_op jit(solution)/shard_map/while/body/eval_jaxpr/ppermute | solution.py:12
  261.3 9.8 %collective-permute-start = (bf16[256,256]{1,0:T(8,128)(2,1)S(1)}, bf16[256,256]{1,0:T(8,128)(2,1)S(1)}, u32[]{:S(2)}, u32[]{:S(2)}) collective-permute-start(bf16[256,256]{1,0:T(8,128)(2,1)S(1)} %copy.47), channel_id=1, source_target_pairs={{0,16},{16,32},{32,48},{48,64},{64,80},{80,96},{96,112},{112,128},... | collective-permute-start | bytes 393224 | tf_op jit(solution)/shard_map/while/body/eval_jaxpr/ppermute | solution.py:12
  271.1 9.8 %collective-permute-start = (bf16[256,256]{1,0:T(8,128)(2,1)S(1)}, bf16[256,256]{1,0:T(8,128)(2,1)S(1)}, u32[]{:S(2)}, u32[]{:S(2)}) collective-permute-start(bf16[256,256]{1,0:T(8,128)(2,1)S(1)} %copy.47), channel_id=1, source_target_pairs={{0,16},{16,32},{32,48},{48,64},{64,80},{80,96},{96,112},{112,128},... | collective-permute-start | bytes 393224 | tf_op jit(solution)/shard_map/while/body/eval_jaxpr/ppermute | solution.py:12
  280.9 9.8 %collective-permute-start = (bf16[256,256]{1,0:T(8,128)(2,1)S(1)}, bf16[256,256]{1,0:T(8,128)(2,1)S(1)}, u32[]{:S(2)}, u32[]{:S(2)}) collective-permute-start(bf16[256,256]{1,0:T(8,128)(2,1)S(1)} %copy.47), channel_id=1, source_target_pairs={{0,16},{16,32},{32,48},{48,64},{64,80},{80,96},{96,112},{112,128},... | collective-permute-start | bytes 393224 | tf_op jit(solution)/shard_map/while/body/eval_jaxpr/ppermute | solution.py:12
  290.7 5.9 %copy-start.5 = (f32[256]{0:T(256)S(1)}, f32[256]{0:T(256)}, u32[]{:S(2)}) copy-start(f32[256]{0:T(256)} %param.16) | copy-start | bytes 3076
Sparse Core Ops, SparseCore 0:
  10.8 43.9 all-gather.4
  57.3 49.6 all-gather.2
  301.5 71.7 reduce-scatter.1
where the time goes:
time: 383 us; the launch traced here: 380 us
  waiting for transfers between devices  124 us (32%)
  local copies, waits for them, and re-layouts  78.9 us (21%)
  other arithmetic  64.1 us (17%)
  matrix products  56.5 us (15%)
  starting transfers between devices  42.1 us (11%)
  between operations  13.3 us (3%)
    reduce_scatter x1, waiting for transfers between devices, per_device(): lax.psum_scatter(lax.dot_general(out_weight, gated, (((0,), (1,)), ((), (...  72 us
    ppermute x16, starting transfers between devices, shifted(): return lax.ppermute(value, axis, pairs)  42 us
    add x15, other arithmetic, absorb(): return total_spec + complex_product(lag_spec, block_spec, half)  33.9 us
    slice x15, local copies, waits for them, and re-layouts, complex_product(): left_re, left_im = (left[..., :half, :], left[..., half:, :])  31.2 us
    dot_general x16, matrix products, absorb(): jnp.dot(forward, block.astype(jnp.float32), precision=lax.Precision.HIGHEST)  29.3 us
    all_gather x1, waiting for transfers between devices, per_device(): lax.all_gather(own_filter.astype(jnp.bfloat16), 'seq', axis=0, tiled=True)  28 us
    all_gather x1, waiting for transfers between devices, per_device(): lax.all_gather(tokens, 'chan', axis=1, tiled=True)  23.5 us
    while x45, local copies, waits for them, and re-layouts  21.6 us
  transfers between devices with their start and end apart: 19, of which 3 were waited for; matrix products, arithmetic and copies ran while one was open for 47% of the time, Pallas kernels for 0%

commit v1 on v0

v1 whole, which is shorter than its diff:
```python
import functools
import math

import jax
import jax.numpy as jnp
import ml_dtypes
import numpy as np
from jax import lax
from jax.experimental import pallas as pl
from jax.experimental.pallas import tpu as pltpu
from jax.sharding import PartitionSpec as P

BLOCK = 256
GROUP = 16
BLOCKS = 16
FREQS = 2 * BLOCK
FEAT_ROWS = 40
MESH_ID = pl.DeviceIdType.MESH
F32 = jnp.float32
BF16 = jnp.bfloat16


def split_two(values):
    high = values.astype(ml_dtypes.bfloat16)
    low = (values - high.astype(np.float64)).astype(ml_dtypes.bfloat16)
    return np.stack([high, low])


@functools.cache
def tables(total):
    row = np.arange(BLOCK)
    freq = np.arange(BLOCK)
    angle = 2.0 * np.pi * ((row[:, None] * freq[None, :]) % FREQS) / FREQS
    imag = -np.sin(angle)
    imag[:, 0] = 1.0 - 2.0 * (row % 2)
    forward = np.concatenate([np.cos(angle), imag], axis=1)
    angle = 2.0 * np.pi * ((freq[:, None] * (row[None, :] + BLOCK)) % FREQS) / FREQS
    real_rows = 2.0 * np.cos(angle)
    real_rows[0] = 1.0
    imag_rows = -2.0 * np.sin(angle)
    imag_rows[0] = 1.0 - 2.0 * (row % 2)
    inverse = np.concatenate([real_rows, imag_rows], axis=0) / FREQS
    place = np.arange(total)
    count = 16
    rates = 1 + np.arange(count) * (total // 4 - 1) // (count - 1)
    phase = (place[None, :] * rates[:, None]) % total
    turn = 2.0 * np.pi * phase / total
    feats = np.zeros((FEAT_ROWS, total), np.float32)
    feats[0] = place / total
    feats[1 : 1 + count] = np.cos(turn)
    feats[1 + count : 1 + 2 * count] = np.sin(turn)
    return split_two(forward), split_two(inverse), feats


def sine(x):
    turns = jnp.round(x * (1.0 / math.pi))
    r = x - turns * 3.140625
    r = r - turns * 0.0009670257568359375
    r = r - turns * 6.2771141529083252e-07
    odd = turns - 2.0 * jnp.floor(turns * 0.5)
    z = r * r
    poly = 1.0 / 6227020800.0
    for term in (-39916800.0, 362880.0, -5040.0, 120.0, -6.0):
        poly = poly * z + 1.0 / term
    value = r + r * z * poly
    return value * (1.0 - 2.0 * odd)


def dot(a, b):
    return jnp.dot(a, b, preferred_element_type=F32)


def halves(x):
    high = x.astype(BF16)
    return high, (x - high.astype(F32)).astype(BF16)


def slot(h, first, second):
    dx, dy = (first, second) if h == 0 else (second, first)
    return (dy % 4) * 4 + dx % 4


def rows(h, part):
    base = h * 128
    return {"f": (base, 128), "q1": (base, 64), "q2": (base + 64, 64)}[part]


class Links:
    def __init__(self, send, recv):
        self.send, self.recv, self.known = send, recv, {}

    def start(self, name, src, dst, device):
        index = len(self.known)
        copy = pltpu.make_async_remote_copy(
            src_ref=src,
            dst_ref=dst,
            send_sem=self.send.at[index],
            recv_sem=self.recv.at[index],
            device_id=device,
            device_id_type=MESH_ID,
        )
        copy.start()
        self.known[name] = copy

    def arrived(self, name):
        self.known[name].wait_recv()

    def finish(self):
        for copy in self.known.values():
            copy.wait_send()


def kernel(
    tok, win, taps, fin, fout, rates, skip, wout, feats, fmat, gmat,
    out,
    xbuf, wbuf, wo, featbuf, fbuf, gbuf, acc, finp, fot, ratecol, skipcol, fs, aspec, sre, sim, sre2,
    pbuf, pf, qbuf, drv, sbuf, dbuf, xs, ys, cbuf, rbuf, gated,
    part, snd, rq, rh, psnd, rpq, rph, red,
    local_sem, w_sem, wo_sem, ag_send, ag_recv, halo_send, halo_recv, a_send, a_recv, b_send, b_recv, rs_send, rs_recv,
):
    s = lax.axis_index("seq")
    c = lax.axis_index("chan")
    x, y = lax.rem(c, 4), lax.div(c, 4)
    spots = [(dx, dy) for dy in range(4) for dx in range(4)]

    def chan_at(dx, dy):
        return lax.rem(y + dy + 4, 4) * 4 + lax.rem(x + dx + 4, 4)

    def neighbour(h, stage, sign):
        along_x = (h == 0) == (stage == 0)
        return {"chan": chan_at(sign, 0) if along_x else chan_at(0, sign)}

    own = pltpu.make_async_copy(tok, xbuf.at[0], local_sem.at[0])
    own.start()
    order = [(0, 0), (1, 0), (3, 0), (0, 1), (0, 3), (2, 0), (0, 2), (1, 1), (1, 3), (3, 1), (3, 3),
             (1, 2), (3, 2), (2, 1), (2, 3), (2, 2)]
    w_copies = {}
    feat_copy = pltpu.make_async_copy(feats, featbuf, local_sem.at[1])
    f_copy = pltpu.make_async_copy(fmat, fbuf, local_sem.at[2])
    g_copy = pltpu.make_async_copy(gmat, gbuf, local_sem.at[3])
    feat_copy.start()
    for n, (dx, dy) in enumerate(order):
        at = pl.ds(pl.multiple_of(chan_at(-dx, -dy) * BLOCK, BLOCK), BLOCK)
        w_copies[dx, dy] = pltpu.make_async_copy(win.at[:, at, :], wbuf.at[n], w_sem.at[n])
        w_copies[dx, dy].start()
        if n == 1:
            f_copy.start()
    g_copy.start()
    wo_copies = {}
    for n, (dx, dy) in enumerate(spots):
        at = pl.ds(pl.multiple_of(chan_at(dx, dy) * BLOCK, BLOCK), BLOCK)
        wo_copies[dx, dy] = pltpu.make_async_copy(wout.at[:, at], wo.at[n], wo_sem.at[n])
        wo_copies[dx, dy].start()

    barrier = pltpu.get_barrier_semaphore()
    for device in (chan_at(1, 0), chan_at(-1, 0), chan_at(0, 1), chan_at(0, -1)):
        pl.semaphore_signal(barrier, inc=1, device_id={"chan": device}, device_id_type=MESH_ID)
    for k in range(1, BLOCKS):
        pl.semaphore_signal(
            barrier, inc=1, device_id={"seq": lax.rem(s + k, BLOCKS)}, device_id_type=MESH_ID
        )
    pl.semaphore_wait(barrier, 4 + BLOCKS - 1)

    links = Links(ag_send, ag_recv)

    def push(name, h, frm, to, piece, stage, sign, src=None):
        start, size = rows(h, piece)
        here = (xbuf.at[slot(h, *frm)] if src is None else src).at[pl.ds(start, size), :]
        there = xbuf.at[slot(h, *to), pl.ds(start, size), :]
        links.start((name, h), here, there, neighbour(h, stage, sign))

    def take(*names):
        for name in names:
            for h in (0, 1):
                links.arrived((name, h))

    def multiply(blocks, first=False):
        for dx, dy in blocks:
            w_copies[dx, dy].wait()
        for j in range(3):
            total = None if first else acc[j]
            for dx, dy in blocks:
                term = dot(xbuf[dy * 4 + dx], wbuf[order.index((dx, dy)), j])
                total = term if total is None else total + term
            acc[j] = total

    for h in (0, 1):
        push("P0+", h, (0, 0), (1, 0), "f", 0, 1, tok)
        push("P0-", h, (0, 0), (3, 0), "f", 0, -1, tok)
    for h in (0, 1):
        push("Q00+", h, (0, 0), (0, 1), "f", 1, 1, tok)
        push("Q00-", h, (0, 0), (0, 3), "f", 1, -1, tok)

    finp[...] = jnp.zeros_like(finp)
    finp[0:33, 0:64] = fin[...]
    fin_t = jnp.transpose(finp[...])[0:64, 0:FEAT_ROWS]
    fot[...] = jnp.transpose(fout[...])
    ratecol[...] = jnp.transpose(jnp.broadcast_to(rates[...], (128, BLOCK)))
    skipcol[...] = jnp.transpose(jnp.broadcast_to(skip[...], (128, BLOCK)))
    mine = pl.ds(pl.multiple_of(s * GROUP, GROUP), GROUP)
    fo = fot[mine, :]
    rate = ratecol[mine, :]
    rate = jnp.concatenate([rate] * 4, axis=1)
    scale = jnp.sqrt(rate)
    feat_copy.wait()

    def filter_piece(n, carry):
        at = pl.ds(pl.multiple_of(n * 512, 512), 512)
        arg = jnp.dot(fin_t, featbuf[:, at], precision=lax.Precision.HIGHEST, preferred_element_type=F32)
        shaped = jnp.dot(fo, sine(arg), precision=lax.Precision.HIGHEST, preferred_element_type=F32)
        place = (lax.broadcasted_iota(jnp.int32, (GROUP, 512), 1) + n * 512).astype(F32)
        value = shaped * scale * jnp.exp(-rate * place)
        fs[pl.ds(pl.multiple_of(n * 32, 32), GROUP), :] = value[:, :BLOCK]
        fs[pl.ds(pl.multiple_of(n * 32 + 16, 16), GROUP), :] = value[:, BLOCK:]
        return carry

    lax.fori_loop(0, 8, filter_piece, 0)
    own.wait()
    multiply([(0, 0)], first=True)

    take("P0+", "P0-")
    for h in (0, 1):
        push("P1+", h, (1, 0), (2, 0), "q1", 0, 1)
        push("P1-", h, (3, 0), (2, 0), "q2", 0, -1)
    for h in (0, 1):
        for dp in (1, 3):
            push(f"Q{dp}0+", h, (dp, 0), (dp, 1), "f", 1, 1)
            push(f"Q{dp}0-", h, (dp, 0), (dp, 3), "f", 1, -1)
    take("Q00+", "Q00-")
    for h in (0, 1):
        push("Q01+", h, (0, 1), (0, 2), "q1", 1, 1)
        push("Q01-", h, (0, 3), (0, 2), "q2", 1, -1)
    multiply([(1, 0), (3, 0), (0, 1), (0, 3)])

    take("P1+", "P1-")
    for h in (0, 1):
        push("Q2a+", h, (2, 0), (2, 1), "q1", 1, 1)
        push("Q2a-", h, (2, 0), (2, 3), "q1", 1, -1)
        push("Q2b+", h, (2, 0), (2, 1), "q2", 1, 1)
        push("Q2b-", h, (2, 0), (2, 3), "q2", 1, -1)

    f_copy.wait()
    high, low = halves(fs[...])
    aspec[0:GROUP, :] = jnp.zeros((GROUP, FREQS), F32)
    aspec[GROUP:, :] = dot(high, fbuf[0]) + dot(low, fbuf[0]) + dot(high, fbuf[1])
    lane = lax.broadcasted_iota(jnp.int32, (GROUP, BLOCK), 1)
    parity = 1.0 - 2.0 * lax.rem(lane, 2).astype(F32)

    def lag_piece(n, carry):
        before = pl.ds(pl.multiple_of(n * GROUP, GROUP), GROUP)
        after = pl.ds(pl.multiple_of(n * GROUP + GROUP, GROUP), GROUP)
        re = aspec[before, 0:BLOCK] + parity * aspec[after, 0:BLOCK]
        im = aspec[before, BLOCK:] + parity * aspec[after, BLOCK:]
        sre[before, :] = re
        sim[before, :] = jnp.where(lane == 0, 0.0, im)
        sre2[before, :] = jnp.where(lane == 0, im, re)
        return carry

    lax.fori_loop(0, BLOCKS, lag_piece, 0)

    for dp in (1, 3):
        take(f"Q{dp}0+", f"Q{dp}0-")
        for h in (0, 1):
            push(f"Q{dp}1+", h, (dp, 1), (dp, 2), "q1", 1, 1)
            push(f"Q{dp}1-", h, (dp, 3), (dp, 2), "q2", 1, -1)
    take("Q01+", "Q01-")
    multiply([(2, 0), (0, 2)])
    take("Q2a+", "Q2b-")
    for h in (0, 1):
        push("Q21+", h, (2, 1), (2, 2), "q1", 1, 1)
        push("Q21-", h, (2, 3), (2, 2), "q2", 1, -1)
    multiply([(1, 1), (1, 3), (3, 1), (3, 3)])
    take("Q2a-", "Q2b+", "Q11+", "Q11-", "Q31+", "Q31-")
    multiply([(1, 2), (3, 2), (2, 1), (2, 3)])
    take("Q21+", "Q21-")
    multiply([(2, 2)])

    for j in range(3):
        rounded = acc[j].astype(BF16)
        pbuf[j, 16:, :] = rounded
        pf[j, 16:, :] = rounded.astype(F32)
    halo = pltpu.make_async_remote_copy(
        src_ref=pbuf.at[:, pl.ds(BLOCK, 16), :],
        dst_ref=pbuf.at[:, pl.ds(0, 16), :],
        send_sem=halo_send.at[0],
        recv_sem=halo_recv.at[0],
        device_id={"seq": lax.rem(s + 1, BLOCKS)},
        device_id_type=MESH_ID,
    )
    halo.start()

    def short(start, size):
        branch = []
        for j in range(3):
            value = taps[0, pl.ds(j, 1), :] * pf[j, pl.ds(16 + start, size), :]
            value = value + taps[1, pl.ds(j, 1), :] * pf[j, pl.ds(15 + start, size), :]
            branch.append(value + taps[2, pl.ds(j, 1), :] * pf[j, pl.ds(14 + start, size), :])
        qbuf[pl.ds(start, size), :] = branch[0]
        drv[pl.ds(start, size), :] = branch[1] * branch[2]

    for start in range(16, BLOCK, 16):
        short(start, 16)
    halo.wait_recv()
    live = (s > 0).astype(F32)
    for j in range(3):
        pf[j, 0:16, :] = pbuf[j, 0:16, :].astype(F32) * live
    short(0, 16)

    sbuf[...] = jnp.transpose(drv[...]).astype(BF16).reshape(BLOCKS, GROUP, BLOCK)

    def exchange(src, dst, send, recv):
        copies = []
        for k in range(1, BLOCKS):
            other = lax.rem(s + k, BLOCKS)
            copy = pltpu.make_async_remote_copy(
                src_ref=src.at[other],
                dst_ref=dst.at[s],
                send_sem=send.at[k],
                recv_sem=recv.at[k],
                device_id={"seq": other},
                device_id_type=MESH_ID,
            )
            copy.start()
            copies.append(copy)
        dst[pl.ds(s, 1)] = src[pl.ds(s, 1)]
        for copy in copies:
            copy.wait_recv()
        return copies

    waits = [halo] + exchange(sbuf, dbuf, a_send, a_recv)

    drive = dbuf[...].reshape(BLOCK, BLOCK)
    xs[...] = dot(drive, fbuf[0]) + dot(drive, fbuf[1])

    def spectrum(i, carry):
        def lag(d, total):
            at = pl.ds(pl.multiple_of((i - d) * GROUP, GROUP), GROUP)
            by = pl.ds(pl.multiple_of(d * GROUP, GROUP), GROUP)
            xr, xi = xs[at, 0:BLOCK], xs[at, BLOCK:]
            im = sim[by, :]
            return (
                total[0] + xr * sre[by, :] - xi * im,
                total[1] + xr * im + xi * sre2[by, :],
            )

        zero = jnp.zeros((GROUP, BLOCK), F32)
        re, im = lax.fori_loop(0, i + 1, lag, (zero, zero))
        to = pl.ds(pl.multiple_of(i * GROUP, GROUP), GROUP)
        ys[to, 0:BLOCK] = re
        ys[to, BLOCK:] = im
        return carry

    lax.fori_loop(0, BLOCKS, spectrum, 0)
    g_copy.wait()
    high, low = halves(ys[...])
    conv = dot(high, gbuf[0]) + dot(low, gbuf[0]) + dot(high, gbuf[1])
    direct = skipcol[mine, :]
    direct = jnp.concatenate([direct, direct], axis=1)
    conv = conv.reshape(BLOCKS, GROUP, BLOCK) + direct[None] * dbuf[...].astype(F32)
    cbuf[...] = conv.astype(BF16)
    waits += exchange(cbuf, rbuf, b_send, b_recv)

    back = jnp.transpose(rbuf[...].reshape(BLOCK, BLOCK).astype(F32))
    gated[...] = (qbuf[...] * back).astype(BF16)

    sums = Links(rs_send, rs_recv)

    def project(dx, dy):
        wo_copies[dx, dy].wait()
        part[dy * 4 + dx] = dot(gated[...], wo[dy * 4 + dx])

    def far(h, dp):
        start, _ = rows(h, "f")
        snd[h, dp, 0] = part[slot(h, dp, 2), pl.ds(start, 128), :].astype(BF16)
        sums.start(("Q1+", h, dp), snd.at[h, dp, 0, pl.ds(0, 64), :], rq.at[h, dp, 0], neighbour(h, 1, 1))
        sums.start(("Q1-", h, dp), snd.at[h, dp, 0, pl.ds(64, 64), :], rq.at[h, dp, 1], neighbour(h, 1, -1))

    project(2, 2)
    far(0, 2)
    far(1, 2)
    for n in (1, 3):
        project(n, 2)
        far(0, n)
        project(2, n)
        far(1, n)
    project(0, 2)
    far(0, 0)
    project(2, 0)
    far(1, 0)
    for dx, dy in ((1, 1), (1, 3), (3, 1), (3, 3), (0, 1), (1, 0), (0, 3), (3, 0), (0, 0)):
        project(dx, dy)

    for dp in (2, 1, 3, 0):
        for h in (0, 1):
            base = h * 128
            sums.arrived(("Q1+", h, dp))
            one = part.at[slot(h, dp, 1)]
            snd[h, dp, 1, 0:64] = (one[pl.ds(base, 64), :] + rq[h, dp, 0].astype(F32)).astype(BF16)
            snd[h, dp, 1, 64:128] = one[pl.ds(base + 64, 64), :].astype(BF16)
            sums.start(("Q2+", h, dp), snd.at[h, dp, 1], rh.at[h, dp, 0], neighbour(h, 1, 1))
            sums.arrived(("Q1-", h, dp))
            one = part.at[slot(h, dp, 3)]
            snd[h, dp, 2, 0:64] = one[pl.ds(base, 64), :].astype(BF16)
            snd[h, dp, 2, 64:128] = (one[pl.ds(base + 64, 64), :] + rq[h, dp, 1].astype(F32)).astype(BF16)
            sums.start(("Q2-", h, dp), snd.at[h, dp, 2], rh.at[h, dp, 1], neighbour(h, 1, -1))

    def reduced(h, dp):
        sums.arrived(("Q2+", h, dp))
        sums.arrived(("Q2-", h, dp))
        return (
            part[slot(h, dp, 0), pl.ds(h * 128, 128), :]
            + rh[h, dp, 0].astype(F32)
            + rh[h, dp, 1].astype(F32)
        )

    for h in (0, 1):
        psnd[h, 0] = reduced(h, 2).astype(BF16)
        sums.start(("P1+", h), psnd.at[h, 0, pl.ds(0, 64), :], rpq.at[h, 0], neighbour(h, 0, 1))
        sums.start(("P1-", h), psnd.at[h, 0, pl.ds(64, 64), :], rpq.at[h, 1], neighbour(h, 0, -1))
    for dp, n in ((1, 0), (3, 1), (0, 2)):
        for h in (0, 1):
            red[h, n] = reduced(h, dp)
    for h in (0, 1):
        sums.arrived(("P1+", h))
        psnd[h, 1, 0:64] = (red[h, 0, 0:64] + rpq[h, 0].astype(F32)).astype(BF16)
        psnd[h, 1, 64:128] = red[h, 0, 64:128].astype(BF16)
        sums.start(("P2+", h), psnd.at[h, 1], rph.at[h, 0], neighbour(h, 0, 1))
        sums.arrived(("P1-", h))
        psnd[h, 2, 0:64] = red[h, 1, 0:64].astype(BF16)
        psnd[h, 2, 64:128] = (red[h, 1, 64:128] + rpq[h, 1].astype(F32)).astype(BF16)
        sums.start(("P2-", h), psnd.at[h, 2], rph.at[h, 1], neighbour(h, 0, -1))
    for h in (0, 1):
        sums.arrived(("P2+", h))
        sums.arrived(("P2-", h))
        total = red[h, 2] + rph[h, 0].astype(F32) + rph[h, 1].astype(F32)
        out[h * 128 : h * 128 + 128, :] = total.astype(BF16)

    links.finish()
    sums.finish()
    for copy in waits:
        copy.wait_send()


def per_device(tokens, in_weight, short_taps, filter_in, filter_out, rates, skip, out_weight):
    forward, inverse, feats = tables(4096)
    vmem = pl.BlockSpec(memory_space=pltpu.VMEM)
    hbm = pl.BlockSpec(memory_space=pl.ANY)
    dma = pltpu.SemaphoreType.DMA
    square = (BLOCK, BLOCK)
    scratch = [
        pltpu.VMEM((16, *square), BF16),
        pltpu.VMEM((16, 3, *square), BF16),
        pltpu.VMEM((16, *square), BF16),
        pltpu.VMEM((FEAT_ROWS, 4096), F32),
        pltpu.VMEM((2, BLOCK, FREQS), BF16),
        pltpu.VMEM((2, FREQS, BLOCK), BF16),
        pltpu.VMEM((3, *square), F32),
        pltpu.VMEM((128, 128), F32),
        pltpu.VMEM((BLOCK, 64), F32),
        pltpu.VMEM((BLOCK, 128), F32),
        pltpu.VMEM((BLOCK, 128), F32),
        pltpu.VMEM(square, F32),
        pltpu.VMEM((GROUP + BLOCK, FREQS), F32),
        pltpu.VMEM(square, F32),
        pltpu.VMEM(square, F32),
        pltpu.VMEM(square, F32),
        pltpu.VMEM((3, 16 + BLOCK, BLOCK), BF16),
        pltpu.VMEM((3, 16 + BLOCK, BLOCK), F32),
        pltpu.VMEM(square, F32),
        pltpu.VMEM(square, F32),
        pltpu.VMEM((BLOCKS, GROUP, BLOCK), BF16),
        pltpu.VMEM((BLOCKS, GROUP, BLOCK), BF16),
        pltpu.VMEM((BLOCK, FREQS), F32),
        pltpu.VMEM((BLOCK, FREQS), F32),
        pltpu.VMEM((BLOCKS, GROUP, BLOCK), BF16),
        pltpu.VMEM((BLOCKS, GROUP, BLOCK), BF16),
        pltpu.VMEM(square, BF16),
        pltpu.VMEM((16, *square), F32),
        pltpu.VMEM((2, 4, 3, 128, BLOCK), BF16),
        pltpu.VMEM((2, 4, 2, 64, BLOCK), BF16),
        pltpu.VMEM((2, 4, 2, 128, BLOCK), BF16),
        pltpu.VMEM((2, 3, 128, BLOCK), BF16),
        pltpu.VMEM((2, 2, 64, BLOCK), BF16),
        pltpu.VMEM((2, 2, 128, BLOCK), BF16),
        pltpu.VMEM((2, 3, 128, BLOCK), F32),
        dma((4,)),
        dma((16,)),
        dma((16,)),
        dma((44,)),
        dma((44,)),
        dma((1,)),
        dma((1,)),
        dma((16,)),
        dma((16,)),
        dma((16,)),
        dma((16,)),
        dma((40,)),
        dma((40,)),
    ]
    return pl.pallas_call(
        kernel,
        out_shape=jax.ShapeDtypeStruct(square, BF16),
        in_specs=[hbm, hbm, vmem, vmem, vmem, vmem, vmem, hbm, hbm, hbm, hbm],
        out_specs=vmem,
        scratch_shapes=scratch,
        compiler_params=pltpu.CompilerParams(
            collective_id=0, has_side_effects=True, vmem_limit_bytes=56 * 1024 * 1024
        ),
        name="hyena",
    )(
        tokens,
        jnp.transpose(in_weight, (1, 0, 2)),
        short_taps,
        filter_in,
        filter_out,
        rates.reshape(1, BLOCK),
        skip.reshape(1, BLOCK),
        out_weight,
        jnp.asarray(feats),
        jnp.asarray(forward),
        jnp.asarray(inverse),
    )


def solution(mesh):
    placed = (
        P("seq", "chan"),
        P(None, None, "chan"),
        P(None, None, "chan"),
        P(),
        P(None, "chan"),
        P("chan"),
        P("chan"),
        P("chan", None),
    )
    return jax.shard_map(
        per_device, mesh=mesh, in_specs=placed, out_specs=P("seq", "chan"), check_vma=False
    )
```

time: 383 us -> 63.7 us (0.17)
  waiting for transfers between devices: 124 us -> 0 us
  local copies, waits for them, and re-layouts: 78.9 us -> 1.57 us
  other arithmetic: 64.1 us -> 0 us
  Pallas kernels: 0 us -> 61.5 us
  matrix products: 56.5 us -> 0 us
  starting transfers between devices: 42.1 us -> 0 us
  between operations: 13.3 us -> 0.01 us
    reduce_scatter x1 -> x0, waiting for transfers between devices: 72 us -> none  [per_device(): lax.psum_scatter(lax.dot_general(out_weight, gated, (((0,), (1,)), ((), (...]
    pallas_call x0 -> x1, Pallas kernels: none -> 61.5 us  [per_device(): pl.pallas_call(kernel, out_shape=jax.ShapeDtypeStruct(square, BF16), in_s...]
    dot_general x22 -> x0, matrix products: 56.5 us -> none  [the longest x16 29.3 us: absorb(): jnp.dot(forward, block.astype(jnp.float32), precision=lax.Precision.HIGHEST)]
    add x20 -> x0, other arithmetic: 51.9 us -> none  [the longest x15 33.9 us: absorb(): return total_spec + complex_product(lag_spec, block_spec, half)]
    all_gather x2 -> x0, waiting for transfers between devices: 51.5 us -> none  [the longest x1 28 us: per_device(): lax.all_gather(own_filter.astype(jnp.bfloat16), 'seq', axis=0, tiled=True)]
    slice x17 -> x0, local copies, waits for them, and re-layouts: 45.8 us -> none  [the longest x15 31.2 us: complex_product(): left_re, left_im = (left[..., :half, :], left[..., half:, :])]
    ppermute x16 -> x0, starting transfers between devices: 42 us -> none  [shifted(): return lax.ppermute(value, axis, pairs)]
    while x46 -> x0, local copies, waits for them, and re-layouts: 23.2 us -> none
  transfers between devices with their start and end apart: 19 -> 0, of which waited for: 3 -> 0; matrix products, arithmetic and copies ran while one was open for 47% -> 0% of each run, Pallas kernels for 0% -> 0%
where the time goes in v1:
time: 63.7 us; the launch traced here: 63.1 us
  Pallas kernels  61.5 us (97%)
  local copies, waits for them, and re-layouts  1.57 us (2%)
    pallas_call x1, Pallas kernels, per_device(): pl.pallas_call(kernel, out_shape=jax.ShapeDtypeStruct(square, BF16), in_s...  61.5 us
    unnamed x1, local copies, waits for them, and re-layouts  1.57 us

profile of v1, /device:TPU:1, one launch (start us, length us, event | category | flops | bytes accessed | tf_op | source)
XLA Modules:
  0.0 63.1 jit_solution(14532650079188278232)
XLA Ops:
  0.0 61.5 %hyena.1 = bf16[256,256]{1,0:T(8,128)(2,1)} custom-call(bf16[256,256]{1,0:T(8,128)(2,1)} %tok.1, bf16[3,4096,256]{2,1,0:T(8,128)(2,1)} %bitcast.3, f32[3,3,256]{2,1,0:T(4,128)} %taps.1, f32[33,64]{1,0:T(8,128)} %fin.1, f32[64,256]{1,0:T(8,128)} %fout.1, f32[1,256]{1,0:T(1,128)} %bitcast.4, f32[1,256]{1,0:T(1,128)} %bitcast.5, bf16[256,4096]{1,0:T(8,128)(2,1)} %wout.1, ...), custom_call_target="tpu_custom_call" | custom-call | tf_op jit(solution)/shard_map/hyena/pallas_call | solution.py:500
  61.5 1.6 %copy.13 = bf16[256,256]{1,0:T(8,128)(2,1)} copy(bf16[256,256]{1,0:T(8,128)(2,1)} %hyena.1) | data formatting | bytes 262144

commit v2 on v1

v2 whole, which is shorter than its diff:
```python
import functools
import math

import jax
import jax.numpy as jnp
import ml_dtypes
import numpy as np
from jax import lax
from jax.experimental import pallas as pl
from jax.experimental.pallas import tpu as pltpu
from jax.sharding import PartitionSpec as P

BLOCK = 256
GROUP = 16
BLOCKS = 16
FREQS = 2 * BLOCK
FEAT_ROWS = 40
EDGE = 16
LAG_STEP = 4
LAG_PAD = (LAG_STEP - 1) * GROUP
ORDER = (8, 7, 9, 6, 10, 5, 11, 4, 12, 3, 13, 2, 14, 1, 15)
MESH_ID = pl.DeviceIdType.MESH
F32 = jnp.float32
BF16 = jnp.bfloat16


def split_two(values):
    high = values.astype(ml_dtypes.bfloat16)
    low = (values - high.astype(np.float64)).astype(ml_dtypes.bfloat16)
    return np.stack([high, low])


@functools.cache
def tables(total):
    row = np.arange(BLOCK)
    freq = np.arange(BLOCK)
    angle = 2.0 * np.pi * ((row[:, None] * freq[None, :]) % FREQS) / FREQS
    imag = -np.sin(angle)
    imag[:, 0] = 1.0 - 2.0 * (row % 2)
    forward = np.concatenate([np.cos(angle), imag], axis=1)
    angle = 2.0 * np.pi * ((freq[:, None] * (row[None, :] + BLOCK)) % FREQS) / FREQS
    real_rows = 2.0 * np.cos(angle)
    real_rows[0] = 1.0
    imag_rows = -2.0 * np.sin(angle)
    imag_rows[0] = 1.0 - 2.0 * (row % 2)
    inverse = np.concatenate([real_rows, imag_rows], axis=0) / FREQS
    place = np.arange(total)
    count = 16
    rates = 1 + np.arange(count) * (total // 4 - 1) // (count - 1)
    phase = (place[None, :] * rates[:, None]) % total
    turn = 2.0 * np.pi * phase / total
    feats = np.zeros((FEAT_ROWS, total), np.float32)
    feats[0] = place / total
    feats[1 : 1 + count] = np.cos(turn)
    feats[1 + count : 1 + 2 * count] = np.sin(turn)
    return split_two(forward), split_two(inverse), feats


def sine(x):
    turns = jnp.round(x * (1.0 / math.pi))
    r = x - turns * 3.140625
    r = r - turns * 0.0009670257568359375
    r = r - turns * 6.2771141529083252e-07
    odd = turns - 2.0 * jnp.floor(turns * 0.5)
    z = r * r
    poly = 1.0 / 6227020800.0
    for term in (-39916800.0, 362880.0, -5040.0, 120.0, -6.0):
        poly = poly * z + 1.0 / term
    value = r + r * z * poly
    return value * (1.0 - 2.0 * odd)


def dot(a, b):
    return jnp.dot(a, b, preferred_element_type=F32)


def halves(x):
    high = x.astype(BF16)
    return high, (x - high.astype(F32)).astype(BF16)


def slot(h, first, second):
    dx, dy = (first, second) if h == 0 else (second, first)
    return (dy % 4) * 4 + dx % 4


def rows(h, part):
    base = h * 128
    cut = EDGE if h else 0
    return {"f": (base, 128 - cut), "q1": (base, 64), "q2": (base + 64, 64 - cut)}[part]


class Links:
    def __init__(self, send, recv):
        self.send, self.recv, self.known = send, recv, {}

    def start(self, name, src, dst, device):
        index = len(self.known)
        copy = pltpu.make_async_remote_copy(
            src_ref=src,
            dst_ref=dst,
            send_sem=self.send.at[index],
            recv_sem=self.recv.at[index],
            device_id=device,
            device_id_type=MESH_ID,
        )
        copy.start()
        self.known[name] = copy

    def arrived(self, name):
        self.known[name].wait_recv()

    def finish(self):
        for copy in self.known.values():
            copy.wait_send()


def kernel(
    tok, win, taps_in, fin_in, fout_in, rates_in, skip_in, wout, feats, fmat, gmat,
    out,
    taps, fin, fout, rates, skip, xbuf, wbuf, wo, featbuf, fbuf, gbuf, acc, finp, fot, ratecol, skipcol, fs, aspec, sre, sim, sre2,
    edge_out, edge_in, pf, qbuf, drv, sbuf, dbuf, xs, ys, cbuf, rbuf, gated,
    part, far_snd, far_rcv, snd, rq, rh, psnd, rp, red,
    word_sem, local_sem, w_sem, wo_sem, ag_send, ag_recv, halo_send, halo_recv, a_send, a_recv, b_send, b_recv, rs_send, rs_recv,
):
    s = lax.axis_index("seq")
    c = lax.axis_index("chan")
    x, y = lax.rem(c, 4), lax.div(c, 4)
    spots = [(dx, dy) for dy in range(4) for dx in range(4)]

    def chan_at(dx, dy):
        return lax.rem(y + dy + 4, 4) * 4 + lax.rem(x + dx + 4, 4)

    def neighbour(h, stage, sign):
        along_x = (h == 0) == (stage == 0)
        return {"chan": chan_at(sign, 0) if along_x else chan_at(0, sign)}

    small = [
        pltpu.make_async_copy(src, dst, local_sem.at[4 + n])
        for n, (src, dst) in enumerate(
            ((fin_in, fin), (fout_in, fout), (rates_in, rates), (skip_in, skip), (taps_in, taps))
        )
    ]
    for copy in small:
        copy.start()
    own = pltpu.make_async_copy(tok, xbuf.at[0], local_sem.at[0])
    own.start()
    order = [(0, 0), (1, 0), (3, 0), (0, 1), (0, 3), (2, 0), (0, 2), (1, 1), (1, 3), (3, 1), (3, 3),
             (1, 2), (2, 1), (3, 2), (2, 3), (2, 2)]
    w_copies = {}
    feat_copy = pltpu.make_async_copy(feats, featbuf, local_sem.at[1])
    f_copy = pltpu.make_async_copy(fmat, fbuf, local_sem.at[2])
    g_copy = pltpu.make_async_copy(gmat, gbuf, local_sem.at[3])
    feat_copy.start()
    for n, (dx, dy) in enumerate(order):
        at = pl.ds(pl.multiple_of(chan_at(-dx, -dy) * BLOCK, BLOCK), BLOCK)
        w_copies[dx, dy] = pltpu.make_async_copy(win.at[:, at, :], wbuf.at[n], w_sem.at[n])
        w_copies[dx, dy].start()
        if n == 1:
            f_copy.start()
    g_copy.start()
    wo_copies = {}
    for n, (dx, dy) in enumerate(spots):
        at = pl.ds(pl.multiple_of(chan_at(dx, dy) * BLOCK, BLOCK), BLOCK)
        wo_copies[dx, dy] = pltpu.make_async_copy(wout.at[:, at], wo.at[n], wo_sem.at[n])
        wo_copies[dx, dy].start()

    z, core = lax.div(s, 2), lax.rem(s, 2)

    def plane(step):
        return {"seq": lax.rem(z + step + 8, 8) * 2 + core}

    sibling = {"seq": z * 2 + 1 - core}
    barrier = pltpu.get_barrier_semaphore()
    near = [{"chan": chan_at(step, 0)} for step in (1, -1, 2)]
    near += [{"chan": chan_at(0, step)} for step in (1, -1, 2)]
    near += [sibling, plane(1), plane(-1)]
    for device in near:
        pl.semaphore_signal(barrier, inc=1, device_id=device, device_id_type=MESH_ID)
    pl.semaphore_wait(barrier, len(near))

    rounds = ([plane(1), plane(-1)], [plane(2), plane(-2)], [sibling])

    def tell(n):
        for device in rounds[n]:
            pl.semaphore_signal(word_sem.at[n], inc=1, device_id=device, device_id_type=MESH_ID)

    def hear(n):
        pl.semaphore_wait(word_sem.at[n], len(rounds[n]))

    links = Links(ag_send, ag_recv)

    def push(name, h, frm, to, piece, stage, sign, src=None):
        start, size = rows(h, piece)
        here = (xbuf.at[slot(h, *frm)] if src is None else src).at[pl.ds(start, size), :]
        there = xbuf.at[slot(h, *to), pl.ds(start, size), :]
        links.start((name, h), here, there, neighbour(h, stage, sign))

    def take(*names):
        for name in names:
            for h in (0, 1):
                links.arrived((name, h))

    def multiply(blocks, first=False):
        for dx, dy in blocks:
            if order.index((dx, dy)) < 3:
                w_copies[dx, dy].wait()
        for j in range(3):
            total = None if first else acc[j]
            for dx, dy in blocks:
                term = dot(xbuf[dy * 4 + dx], wbuf[order.index((dx, dy)), j])
                total = term if total is None else total + term
            acc[j] = total

    tell(0)
    for h in (0, 1):
        push("P2", h, (0, 0), (2, 0), "f", 0, 2, tok)
        push("P0+", h, (0, 0), (1, 0), "f", 0, 1, tok)
        push("P0-", h, (0, 0), (3, 0), "f", 0, -1, tok)
    edge = pl.ds(BLOCK - EDGE, EDGE)
    for step in (1, 2, 3):
        links.start(("EP", step), tok.at[edge, :], xbuf.at[step, edge, :], {"chan": chan_at(step, 0)})
    for h in (0, 1):
        push("Q00+", h, (0, 0), (0, 1), "f", 1, 1, tok)
        push("Q00-", h, (0, 0), (0, 3), "f", 1, -1, tok)

    for copy in small:
        copy.wait()
    finp[...] = jnp.zeros_like(finp)
    finp[0:33, 0:64] = fin[...]
    fin_t = jnp.transpose(finp[...])[0:64, 0:FEAT_ROWS]
    fot[...] = jnp.transpose(fout[...])
    ratecol[...] = jnp.transpose(jnp.broadcast_to(rates[...], (128, BLOCK)))
    skipcol[...] = jnp.transpose(jnp.broadcast_to(skip[...], (128, BLOCK)))
    mine = pl.ds(pl.multiple_of(s * GROUP, GROUP), GROUP)
    fo = fot[mine, :]
    rate = ratecol[mine, :]
    rate = jnp.concatenate([rate] * 4, axis=1)
    scale = jnp.sqrt(rate)
    feat_copy.wait()

    def filter_piece(n, carry):
        at = pl.ds(pl.multiple_of(n * 512, 512), 512)
        arg = jnp.dot(fin_t, featbuf[:, at], precision=lax.Precision.HIGHEST, preferred_element_type=F32)
        shaped = jnp.dot(fo, sine(arg), precision=lax.Precision.HIGHEST, preferred_element_type=F32)
        place = (lax.broadcasted_iota(jnp.int32, (GROUP, 512), 1) + n * 512).astype(F32)
        value = shaped * scale * jnp.exp(-rate * place)
        fs[pl.ds(pl.multiple_of(n * 32, 32), GROUP), :] = value[:, :BLOCK]
        fs[pl.ds(pl.multiple_of(n * 32 + 16, 16), GROUP), :] = value[:, BLOCK:]
        return carry

    lax.fori_loop(0, 8, filter_piece, 0)
    own.wait()
    multiply([(0, 0)], first=True)

    take("P0+", "P0-")
    for h in (0, 1):
        for dp in (1, 3):
            push(f"Q{dp}0+", h, (dp, 0), (dp, 1), "f", 1, 1)
            push(f"Q{dp}0-", h, (dp, 0), (dp, 3), "f", 1, -1)
    for step in (1, 2, 3):
        links.arrived(("EP", step))
    row = xbuf.at[pl.ds(0, 4), edge, :]
    for step in (1, 2, 3):
        links.start(("EQ", step), row, xbuf.at[pl.ds(4 * step, 4), edge, :], {"chan": chan_at(0, step)})
    take("P2")
    for h in (0, 1):
        push("Q20+", h, (2, 0), (2, 1), "f", 1, 1)
        push("Q20-", h, (2, 0), (2, 3), "f", 1, -1)
    take("Q00+", "Q00-")
    for h in (0, 1):
        push("Q01+", h, (0, 1), (0, 2), "q1", 1, 1)
        push("Q01-", h, (0, 3), (0, 2), "q2", 1, -1)
    hear(0)
    tell(1)
    multiply([(1, 0), (3, 0)])
    for dp in (1, 3):
        take(f"Q{dp}0+", f"Q{dp}0-")
        for h in (0, 1):
            push(f"Q{dp}1+", h, (dp, 1), (dp, 2), "q1", 1, 1)
            push(f"Q{dp}1-", h, (dp, 3), (dp, 2), "q2", 1, -1)

    for step in (1, 2, 3):
        links.arrived(("EQ", step))
    for dx, dy in order[3:]:
        w_copies[dx, dy].wait()
    for j in range(3):
        total = None
        for dx, dy in order:
            term = dot(xbuf[dy * 4 + dx, BLOCK - EDGE :, :], wbuf[order.index((dx, dy)), j])
            total = term if total is None else total + term
        edge_out[j] = total.astype(BF16)
    halo = pltpu.make_async_remote_copy(
        src_ref=edge_out,
        dst_ref=edge_in,
        send_sem=halo_send.at[0],
        recv_sem=halo_recv.at[0],
        device_id={"seq": lax.rem(s + 1, BLOCKS)},
        device_id_type=MESH_ID,
    )
    halo.start()
    hear(1)
    tell(2)
    take("Q20+", "Q20-")
    for h in (0, 1):
        push("Q21+", h, (2, 1), (2, 2), "q1", 1, 1)
        push("Q21-", h, (2, 3), (2, 2), "q2", 1, -1)

    f_copy.wait()
    high, low = halves(fs[...])
    aspec[0:GROUP, :] = jnp.zeros((GROUP, FREQS), F32)
    aspec[GROUP:, :] = dot(high, fbuf[0]) + dot(low, fbuf[0]) + dot(high, fbuf[1])
    lane = lax.broadcasted_iota(jnp.int32, (GROUP, BLOCK), 1)
    parity = 1.0 - 2.0 * lax.rem(lane, 2).astype(F32)

    for table in (sre, sim, sre2):
        table[BLOCK:, :] = jnp.zeros((LAG_PAD, BLOCK), F32)

    def lag_piece(n, carry):
        before = pl.ds(pl.multiple_of(n * GROUP, GROUP), GROUP)
        after = pl.ds(pl.multiple_of(n * GROUP + GROUP, GROUP), GROUP)
        re = aspec[before, 0:BLOCK] + parity * aspec[after, 0:BLOCK]
        im = aspec[before, BLOCK:] + parity * aspec[after, BLOCK:]
        sre[before, :] = re
        sim[before, :] = jnp.where(lane == 0, 0.0, im)
        sre2[before, :] = jnp.where(lane == 0, im, re)
        return carry

    lax.fori_loop(0, BLOCKS, lag_piece, 0)

    take("Q01+", "Q01-")
    multiply([(0, 1), (0, 3), (2, 0), (0, 2), (1, 1), (1, 3), (3, 1), (3, 3)])
    for h, dp, block in ((0, 1, (1, 2)), (1, 1, (2, 1)), (0, 3, (3, 2)), (1, 3, (2, 3))):
        links.arrived((f"Q{dp}1+", h))
        links.arrived((f"Q{dp}1-", h))
        multiply([block])
    hear(2)
    take("Q21+", "Q21-")
    multiply([(2, 2)])

    for j in range(3):
        pf[j, 16:, :] = acc[j].astype(BF16).astype(F32)

    def short(start, size):
        branch = []
        for j in range(3):
            value = taps[0, pl.ds(j, 1), :] * pf[j, pl.ds(16 + start, size), :]
            value = value + taps[1, pl.ds(j, 1), :] * pf[j, pl.ds(15 + start, size), :]
            branch.append(value + taps[2, pl.ds(j, 1), :] * pf[j, pl.ds(14 + start, size), :])
        qbuf[pl.ds(start, size), :] = branch[0]
        drv[pl.ds(start, size), :] = branch[1] * branch[2]

    halo.wait_recv()
    live = (s > 0).astype(F32)
    for j in range(3):
        pf[j, 0:16, :] = edge_in[j].astype(F32) * live
    for start in range(0, BLOCK, 32):
        short(start, 32)

    sbuf[...] = jnp.transpose(drv[...]).astype(BF16).reshape(BLOCKS, GROUP, BLOCK)

    def give(k, src, dst, send, recv):
        other = lax.rem(s + k, BLOCKS)
        copy = pltpu.make_async_remote_copy(
            src_ref=src,
            dst_ref=dst.at[s],
            send_sem=send.at[k],
            recv_sem=recv.at[k],
            device_id={"seq": other},
            device_id_type=MESH_ID,
        )
        copy.start()
        return copy

    gone = [give(k, sbuf.at[lax.rem(s + k, BLOCKS)], dbuf, a_send, a_recv) for k in ORDER]
    dbuf[pl.ds(s, 1)] = sbuf[pl.ds(s, 1)]
    xs[0:LAG_PAD, :] = jnp.zeros((LAG_PAD, FREQS), F32)
    direct = skipcol[mine, :]
    direct = jnp.concatenate([direct, direct], axis=1)
    g_copy.wait()
    for copy in gone:
        copy.wait_recv()
    waits = [halo] + gone

    drive = dbuf[...].reshape(BLOCK, BLOCK)
    xs[LAG_PAD:, :] = dot(drive, fbuf[0]) + dot(drive, fbuf[1])

    def spectrum(n, i):
        def lags(turn, total):
            re, im = total
            for d in range(LAG_STEP):
                d = turn * LAG_STEP + d
                at = pl.ds(pl.multiple_of((i - d) * GROUP + LAG_PAD, GROUP), GROUP)
                by = pl.ds(pl.multiple_of(d * GROUP, GROUP), GROUP)
                xr, xi = xs[at, 0:BLOCK], xs[at, BLOCK:]
                part_im = sim[by, :]
                re = re + (xr * sre[by, :] - xi * part_im)
                im = im + (xr * part_im + xi * sre2[by, :])
            return re, im

        zero = jnp.zeros((GROUP, BLOCK), F32)
        re, im = lax.fori_loop(0, lax.div(i + LAG_STEP, LAG_STEP), lags, (zero, zero))
        ys[n * GROUP : (n + 1) * GROUP, 0:BLOCK] = re
        ys[n * GROUP : (n + 1) * GROUP, BLOCK:] = im

    steps = ORDER + (0,)
    for start in (0, 8):
        for n in range(start, start + 8):
            spectrum(n, lax.rem(s + steps[n], BLOCKS))
        some = slice(start * GROUP, start * GROUP + 8 * GROUP)
        high, low = halves(ys[some, :])
        both = dot(jnp.concatenate([high, low], axis=0), gbuf[0])
        conv = both[: 8 * GROUP] + both[8 * GROUP :] + dot(high, gbuf[1])
        for n in range(start, start + 8):
            i = lax.rem(s + steps[n], BLOCKS)
            value = conv[(n - start) * GROUP : (n - start + 1) * GROUP, :]
            cbuf[n] = (value + direct * dbuf[i].astype(F32)).astype(BF16)
            if steps[n]:
                waits.append(give(steps[n], cbuf.at[n], rbuf, b_send, b_recv))
    rbuf[pl.ds(s, 1)] = cbuf[pl.ds(BLOCKS - 1, 1)]
    for copy in waits[-15:]:
        copy.wait_recv()

    back = jnp.transpose(rbuf[...].reshape(BLOCK, BLOCK).astype(F32))
    gated[...] = (qbuf[...] * back).astype(BF16)

    sums = Links(rs_send, rs_recv)

    def project(dx, dy):
        wo_copies[dx, dy].wait()
        part[dy * 4 + dx] = dot(gated[...], wo[dy * 4 + dx])

    def half(h, dp, dq):
        return part.at[slot(h, dp, dq), pl.ds(h * 128, 128), :]

    def straight(h, n):
        dq, sign = ((2, 2), (1, 1), (3, -1))[n]
        far_snd[h, n] = half(h, 2, dq)[...].astype(BF16)
        sums.start(("F", h, n), far_snd.at[h, n], far_rcv.at[h, n], neighbour(h, 1, sign))

    def relay(h, e):
        snd[h, e, 0] = half(h, (1, 3, 0)[e], 2)[...].astype(BF16)
        sums.start(("Q1+", h, e), snd.at[h, e, 0, pl.ds(0, 64), :], rq.at[h, e, 0], neighbour(h, 1, 1))
        sums.start(("Q1-", h, e), snd.at[h, e, 0, pl.ds(64, 64), :], rq.at[h, e, 1], neighbour(h, 1, -1))

    for n in (1, 3):
        project(n, 2)
        relay(0, (n - 1) // 2)
        project(2, n)
        relay(1, (n - 1) // 2)
    project(2, 2)
    for h in (0, 1):
        for n in (0, 1, 2):
            straight(h, n)
    project(0, 2)
    relay(0, 2)
    project(2, 0)
    relay(1, 2)
    for dx, dy in ((1, 1), (1, 3), (3, 1), (3, 3), (0, 1), (1, 0), (0, 3), (3, 0), (0, 0)):
        project(dx, dy)

    for e in (0, 1, 2):
        dp = (1, 3, 0)[e]
        for h in (0, 1):
            sums.arrived(("Q1+", h, e))
            one = half(h, dp, 1)
            snd[h, e, 1, 0:64] = (one[0:64, :] + rq[h, e, 0].astype(F32)).astype(BF16)
            snd[h, e, 1, 64:128] = one[64:128, :].astype(BF16)
            sums.start(("Q2+", h, e), snd.at[h, e, 1], rh.at[h, e, 0], neighbour(h, 1, 1))
            sums.arrived(("Q1-", h, e))
            one = half(h, dp, 3)
            snd[h, e, 2, 0:64] = one[0:64, :].astype(BF16)
            snd[h, e, 2, 64:128] = (one[64:128, :] + rq[h, e, 1].astype(F32)).astype(BF16)
            sums.start(("Q2-", h, e), snd.at[h, e, 2], rh.at[h, e, 1], neighbour(h, 1, -1))
    for h in (0, 1):
        total = half(h, 2, 0)[...]
        for n in (1, 2, 0):
            sums.arrived(("F", h, n))
            total = total + far_rcv[h, n].astype(F32)
        psnd[h, 0] = total.astype(BF16)
        sums.start(("P", h, 0), psnd.at[h, 0], rp.at[h, 0], neighbour(h, 0, 2))

    def reduced(h, e):
        sums.arrived(("Q2+", h, e))
        sums.arrived(("Q2-", h, e))
        return half(h, (1, 3, 0)[e], 0)[...] + rh[h, e, 0].astype(F32) + rh[h, e, 1].astype(F32)

    for e, sign in ((0, 1), (1, -1)):
        for h in (0, 1):
            psnd[h, 1 + e] = reduced(h, e).astype(BF16)
            sums.start(("P", h, 1 + e), psnd.at[h, 1 + e], rp.at[h, 1 + e], neighbour(h, 0, sign))
    for h in (0, 1):
        red[h] = reduced(h, 2)
    for h in (0, 1):
        total = red[h]
        for n in (0, 1, 2):
            sums.arrived(("P", h, n))
            total = total + rp[h, n].astype(F32)
        out[h * 128 : h * 128 + 128, :] = total.astype(BF16)

    links.finish()
    sums.finish()
    for copy in waits:
        copy.wait_send()


def per_device(tokens, in_weight, short_taps, filter_in, filter_out, rates, skip, out_weight):
    forward, inverse, feats = tables(4096)
    vmem = pl.BlockSpec(memory_space=pltpu.VMEM)
    hbm = pl.BlockSpec(memory_space=pl.ANY)
    dma = pltpu.SemaphoreType.DMA
    square = (BLOCK, BLOCK)
    scratch = [
        pltpu.VMEM((3, 3, BLOCK), F32),
        pltpu.VMEM((33, 64), F32),
        pltpu.VMEM((64, BLOCK), F32),
        pltpu.VMEM((1, BLOCK), F32),
        pltpu.VMEM((1, BLOCK), F32),
        pltpu.VMEM((16, *square), BF16),
        pltpu.VMEM((16, 3, *square), BF16),
        pltpu.VMEM((16, *square), BF16),
        pltpu.VMEM((FEAT_ROWS, 4096), F32),
        pltpu.VMEM((2, BLOCK, FREQS), BF16),
        pltpu.VMEM((2, FREQS, BLOCK), BF16),
        pltpu.VMEM((3, *square), F32),
        pltpu.VMEM((128, 128), F32),
        pltpu.VMEM((BLOCK, 64), F32),
        pltpu.VMEM((BLOCK, 128), F32),
        pltpu.VMEM((BLOCK, 128), F32),
        pltpu.VMEM(square, F32),
        pltpu.VMEM((GROUP + BLOCK, FREQS), F32),
        pltpu.VMEM((BLOCK + LAG_PAD, BLOCK), F32),
        pltpu.VMEM((BLOCK + LAG_PAD, BLOCK), F32),
        pltpu.VMEM((BLOCK + LAG_PAD, BLOCK), F32),
        pltpu.VMEM((3, EDGE, BLOCK), BF16),
        pltpu.VMEM((3, EDGE, BLOCK), BF16),
        pltpu.VMEM((3, 16 + BLOCK, BLOCK), F32),
        pltpu.VMEM(square, F32),
        pltpu.VMEM(square, F32),
        pltpu.VMEM((BLOCKS, GROUP, BLOCK), BF16),
        pltpu.VMEM((BLOCKS, GROUP, BLOCK), BF16),
        pltpu.VMEM((LAG_PAD + BLOCK, FREQS), F32),
        pltpu.VMEM((BLOCK, FREQS), F32),
        pltpu.VMEM((BLOCKS, GROUP, BLOCK), BF16),
        pltpu.VMEM((BLOCKS, GROUP, BLOCK), BF16),
        pltpu.VMEM(square, BF16),
        pltpu.VMEM((16, *square), F32),
        pltpu.VMEM((2, 3, 128, BLOCK), BF16),
        pltpu.VMEM((2, 3, 128, BLOCK), BF16),
        pltpu.VMEM((2, 3, 3, 128, BLOCK), BF16),
        pltpu.VMEM((2, 3, 2, 64, BLOCK), BF16),
        pltpu.VMEM((2, 3, 2, 128, BLOCK), BF16),
        pltpu.VMEM((2, 3, 128, BLOCK), BF16),
        pltpu.VMEM((2, 3, 128, BLOCK), BF16),
        pltpu.VMEM((2, 128, BLOCK), F32),
        pltpu.SemaphoreType.REGULAR((3,)),
        dma((9,)),
        dma((16,)),
        dma((16,)),
        dma((44,)),
        dma((44,)),
        dma((1,)),
        dma((1,)),
        dma((16,)),
        dma((16,)),
        dma((16,)),
        dma((16,)),
        dma((36,)),
        dma((36,)),
    ]
    return pl.pallas_call(
        kernel,
        out_shape=jax.ShapeDtypeStruct(square, BF16),
        in_specs=[hbm] * 11,
        out_specs=vmem,
        scratch_shapes=scratch,
        compiler_params=pltpu.CompilerParams(
            collective_id=0, has_side_effects=True, vmem_limit_bytes=56 * 1024 * 1024
        ),
        name="hyena",
    )(
        tokens,
        jnp.transpose(in_weight, (1, 0, 2)),
        short_taps,
        filter_in,
        filter_out,
        rates.reshape(1, BLOCK),
        skip.reshape(1, BLOCK),
        out_weight,
        jnp.asarray(feats),
        jnp.asarray(forward),
        jnp.asarray(inverse),
    )


def solution(mesh):
    placed = (
        P("seq", "chan"),
        P(None, None, "chan"),
        P(None, None, "chan"),
        P(),
        P(None, "chan"),
        P("chan"),
        P("chan"),
        P("chan", None),
    )
    return jax.shard_map(
        per_device, mesh=mesh, in_specs=placed, out_specs=P("seq", "chan"), check_vma=False
    )
```

time: 63.7 us -> 59.4 us (0.932)
  Pallas kernels: 61.5 us -> 57.7 us
    pallas_call x1, Pallas kernels: 61.5 us -> 57.7 us  [per_device(): pl.pallas_call(kernel, out_shape=jax.ShapeDtypeStruct(square, BF16), in_s...]
where the time goes in v2:
time: 59.4 us; the launch traced here: 59.3 us
  Pallas kernels  57.7 us (97%)
  local copies, waits for them, and re-layouts  1.57 us (3%)
    pallas_call x1, Pallas kernels, per_device(): pl.pallas_call(kernel, out_shape=jax.ShapeDtypeStruct(square, BF16), in_s...  57.7 us
    unnamed x1, local copies, waits for them, and re-layouts  1.57 us

profile of v2, /device:TPU:1, one launch (start us, length us, event | category | flops | bytes accessed | tf_op | source)
XLA Modules:
  0.0 59.3 jit_solution(10783691203796742804)
XLA Ops:
  0.0 57.7 %hyena.1 = bf16[256,256]{1,0:T(8,128)(2,1)} custom-call(bf16[256,256]{1,0:T(8,128)(2,1)} %tok.1, bf16[3,4096,256]{2,1,0:T(8,128)(2,1)} %bitcast.3, f32[3,3,256]{2,1,0:T(4,128)} %taps_in.1, f32[33,64]{1,0:T(8,128)} %fin_in.1, f32[64,256]{1,0:T(8,128)} %fout_in.1, f32[1,256]{1,0:T(1,128)} %bitcast.4, f32[1,256]{1,0:T(1,128)} %bitcast.5, ...), custom_call_target="tpu_custom_call" | custom-call | tf_op jit(solution)/shard_map/hyena/pallas_call | solution.py:571
  57.7 1.6 %copy.13 = bf16[256,256]{1,0:T(8,128)(2,1)} copy(bf16[256,256]{1,0:T(8,128)(2,1)} %hyena.1) | data formatting | bytes 262144

commit v3 on v2

--- a/solution.py
+++ b/solution.py
@@ -120,7 +120,7 @@
     out,
     taps, fin, fout, rates, skip, xbuf, wbuf, wo, featbuf, fbuf, gbuf, acc, finp, fot, ratecol, skipcol, fs, aspec, sre, sim, sre2,
     edge_out, edge_in, pf, qbuf, drv, sbuf, dbuf, xs, ys, cbuf, rbuf, gated,
-    part, far_snd, far_rcv, snd, rq, rh, psnd, rp, red,
+    part, snd, rq, rh, psnd, rp, red,
     word_sem, local_sem, w_sem, wo_sem, ag_send, ag_recv, halo_send, halo_recv, a_send, a_recv, b_send, b_recv, rs_send, rs_recv,
 ):
     s = lax.axis_index("seq")
@@ -134,6 +134,19 @@
     def neighbour(h, stage, sign):
         along_x = (h == 0) == (stage == 0)
         return {"chan": chan_at(sign, 0) if along_x else chan_at(0, sign)}
+
+    z, core = lax.div(s, 2), lax.rem(s, 2)
+
+    def plane(step):
+        return {"seq": lax.rem(z + step + 8, 8) * 2 + core}
+
+    sibling = {"seq": z * 2 + 1 - core}
+    barrier = pltpu.get_barrier_semaphore()
+    near = [{"chan": chan_at(step, 0)} for step in (1, -1, 2)]
+    near += [{"chan": chan_at(0, step)} for step in (1, -1, 2)]
+    near += [sibling, plane(1), plane(-1)]
+    for device in near:
+        pl.semaphore_signal(barrier, inc=1, device_id=device, device_id_type=MESH_ID)
 
     small = [
         pltpu.make_async_copy(src, dst, local_sem.at[4 + n])
@@ -152,31 +165,17 @@
     f_copy = pltpu.make_async_copy(fmat, fbuf, local_sem.at[2])
     g_copy = pltpu.make_async_copy(gmat, gbuf, local_sem.at[3])
     feat_copy.start()
-    for n, (dx, dy) in enumerate(order):
-        at = pl.ds(pl.multiple_of(chan_at(-dx, -dy) * BLOCK, BLOCK), BLOCK)
-        w_copies[dx, dy] = pltpu.make_async_copy(win.at[:, at, :], wbuf.at[n], w_sem.at[n])
-        w_copies[dx, dy].start()
-        if n == 1:
-            f_copy.start()
-    g_copy.start()
+
+    def start_weights(first, last):
+        for n in range(first, last):
+            dx, dy = order[n]
+            at = pl.ds(pl.multiple_of(chan_at(-dx, -dy) * BLOCK, BLOCK), BLOCK)
+            w_copies[dx, dy] = pltpu.make_async_copy(win.at[:, at, :], wbuf.at[n], w_sem.at[n])
+            w_copies[dx, dy].start()
+
+    start_weights(0, 1)
     wo_copies = {}
-    for n, (dx, dy) in enumerate(spots):
-        at = pl.ds(pl.multiple_of(chan_at(dx, dy) * BLOCK, BLOCK), BLOCK)
-        wo_copies[dx, dy] = pltpu.make_async_copy(wout.at[:, at], wo.at[n], wo_sem.at[n])
-        wo_copies[dx, dy].start()
-
-    z, core = lax.div(s, 2), lax.rem(s, 2)
-
-    def plane(step):
-        return {"seq": lax.rem(z + step + 8, 8) * 2 + core}
-
-    sibling = {"seq": z * 2 + 1 - core}
-    barrier = pltpu.get_barrier_semaphore()
-    near = [{"chan": chan_at(step, 0)} for step in (1, -1, 2)]
-    near += [{"chan": chan_at(0, step)} for step in (1, -1, 2)]
-    near += [sibling, plane(1), plane(-1)]
-    for device in near:
-        pl.semaphore_signal(barrier, inc=1, device_id=device, device_id_type=MESH_ID)
+
     pl.semaphore_wait(barrier, len(near))
 
     rounds = ([plane(1), plane(-1)], [plane(2), plane(-2)], [sibling])
@@ -190,9 +189,9 @@
 
     links = Links(ag_send, ag_recv)
 
-    def push(name, h, frm, to, piece, stage, sign, src=None):
+    def push(name, h, frm, to, piece, stage, sign):
         start, size = rows(h, piece)
-        here = (xbuf.at[slot(h, *frm)] if src is None else src).at[pl.ds(start, size), :]
+        here = xbuf.at[slot(h, *frm), pl.ds(start, size), :]
         there = xbuf.at[slot(h, *to), pl.ds(start, size), :]
         links.start((name, h), here, there, neighbour(h, stage, sign))
 
@@ -203,7 +202,7 @@
 
     def multiply(blocks, first=False):
         for dx, dy in blocks:
-            if order.index((dx, dy)) < 3:
+            if (dx, dy) == (0, 0):
                 w_copies[dx, dy].wait()
         for j in range(3):
             total = None if first else acc[j]
@@ -212,17 +211,26 @@
                 total = term if total is None else total + term
             acc[j] = total
 
+    own.wait()
     tell(0)
     for h in (0, 1):
-        push("P2", h, (0, 0), (2, 0), "f", 0, 2, tok)
-        push("P0+", h, (0, 0), (1, 0), "f", 0, 1, tok)
-        push("P0-", h, (0, 0), (3, 0), "f", 0, -1, tok)
+        push("P2", h, (0, 0), (2, 0), "f", 0, 2)
+        push("P0+", h, (0, 0), (1, 0), "f", 0, 1)
+        push("P0-", h, (0, 0), (3, 0), "f", 0, -1)
+    for h in (0, 1):
+        push("Q00+", h, (0, 0), (0, 1), "f", 1, 1)
+        push("Q00-", h, (0, 0), (0, 3), "f", 1, -1)
+
     edge = pl.ds(BLOCK - EDGE, EDGE)
     for step in (1, 2, 3):
-        links.start(("EP", step), tok.at[edge, :], xbuf.at[step, edge, :], {"chan": chan_at(step, 0)})
-    for h in (0, 1):
-        push("Q00+", h, (0, 0), (0, 1), "f", 1, 1, tok)
-        push("Q00-", h, (0, 0), (0, 3), "f", 1, -1, tok)
+        links.start(
+            ("EP", step),
+            xbuf.at[0, edge, :],
+            xbuf.at[step * (1 + 3 * core), edge, :],
+            {"chan": chan_at(step * (1 - core), step * core)},
+        )
+    start_weights(1, 16)
+    f_copy.start()
 
     for copy in small:
         copy.wait()
@@ -249,8 +257,7 @@
         fs[pl.ds(pl.multiple_of(n * 32 + 16, 16), GROUP), :] = value[:, BLOCK:]
         return carry
 
-    lax.fori_loop(0, 8, filter_piece, 0)
-    own.wait()
+    lax.fori_loop(0, 4, filter_piece, 0)
     multiply([(0, 0)], first=True)
 
     take("P0+", "P0-")
@@ -258,11 +265,6 @@
         for dp in (1, 3):
             push(f"Q{dp}0+", h, (dp, 0), (dp, 1), "f", 1, 1)
             push(f"Q{dp}0-", h, (dp, 0), (dp, 3), "f", 1, -1)
-    for step in (1, 2, 3):
-        links.arrived(("EP", step))
-    row = xbuf.at[pl.ds(0, 4), edge, :]
-    for step in (1, 2, 3):
-        links.start(("EQ", step), row, xbuf.at[pl.ds(4 * step, 4), edge, :], {"chan": chan_at(0, step)})
     take("P2")
     for h in (0, 1):
         push("Q20+", h, (2, 0), (2, 1), "f", 1, 1)
@@ -271,18 +273,34 @@
     for h in (0, 1):
         push("Q01+", h, (0, 1), (0, 2), "q1", 1, 1)
         push("Q01-", h, (0, 3), (0, 2), "q2", 1, -1)
+    for step in (1, 2, 3):
+        links.arrived(("EP", step))
+    for step in (1, 2, 3):
+        for k in range(4):
+            links.start(
+                ("EQ", step, k),
+                xbuf.at[k * (1 + 3 * core), edge, :],
+                xbuf.at[k * (1 + 3 * core) + step * (4 - 3 * core), edge, :],
+                {"chan": chan_at(step * core, step * (1 - core))},
+            )
     hear(0)
     tell(1)
-    multiply([(1, 0), (3, 0)])
+    lax.fori_loop(4, 8, filter_piece, 0)
     for dp in (1, 3):
         take(f"Q{dp}0+", f"Q{dp}0-")
         for h in (0, 1):
             push(f"Q{dp}1+", h, (dp, 1), (dp, 2), "q1", 1, 1)
             push(f"Q{dp}1-", h, (dp, 3), (dp, 2), "q2", 1, -1)
 
+    take("Q20+", "Q20-")
+    for h in (0, 1):
+        push("Q21+", h, (2, 1), (2, 2), "q1", 1, 1)
+        push("Q21-", h, (2, 3), (2, 2), "q2", 1, -1)
+
     for step in (1, 2, 3):
-        links.arrived(("EQ", step))
-    for dx, dy in order[3:]:
+        for k in range(4):
+            links.arrived(("EQ", step, k))
+    for dx, dy in order[1:]:
         w_copies[dx, dy].wait()
     for j in range(3):
         total = None
@@ -301,35 +319,14 @@
     halo.start()
     hear(1)
     tell(2)
-    take("Q20+", "Q20-")
-    for h in (0, 1):
-        push("Q21+", h, (2, 1), (2, 2), "q1", 1, 1)
-        push("Q21-", h, (2, 3), (2, 2), "q2", 1, -1)
-
-    f_copy.wait()
-    high, low = halves(fs[...])
-    aspec[0:GROUP, :] = jnp.zeros((GROUP, FREQS), F32)
-    aspec[GROUP:, :] = dot(high, fbuf[0]) + dot(low, fbuf[0]) + dot(high, fbuf[1])
-    lane = lax.broadcasted_iota(jnp.int32, (GROUP, BLOCK), 1)
-    parity = 1.0 - 2.0 * lax.rem(lane, 2).astype(F32)
-
-    for table in (sre, sim, sre2):
-        table[BLOCK:, :] = jnp.zeros((LAG_PAD, BLOCK), F32)
-
-    def lag_piece(n, carry):
-        before = pl.ds(pl.multiple_of(n * GROUP, GROUP), GROUP)
-        after = pl.ds(pl.multiple_of(n * GROUP + GROUP, GROUP), GROUP)
-        re = aspec[before, 0:BLOCK] + parity * aspec[after, 0:BLOCK]
-        im = aspec[before, BLOCK:] + parity * aspec[after, BLOCK:]
-        sre[before, :] = re
-        sim[before, :] = jnp.where(lane == 0, 0.0, im)
-        sre2[before, :] = jnp.where(lane == 0, im, re)
-        return carry
-
-    lax.fori_loop(0, BLOCKS, lag_piece, 0)
+    g_copy.start()
+    for n, (dx, dy) in enumerate(spots):
+        at = pl.ds(pl.multiple_of(chan_at(dx, dy) * BLOCK, BLOCK), BLOCK)
+        wo_copies[dx, dy] = pltpu.make_async_copy(wout.at[:, at], wo.at[n], wo_sem.at[n])
+        wo_copies[dx, dy].start()
 
     take("Q01+", "Q01-")
-    multiply([(0, 1), (0, 3), (2, 0), (0, 2), (1, 1), (1, 3), (3, 1), (3, 3)])
+    multiply(order[1:11])
     for h, dp, block in ((0, 1, (1, 2)), (1, 1, (2, 1)), (0, 3, (3, 2)), (1, 3, (2, 3))):
         links.arrived((f"Q{dp}1+", h))
         links.arrived((f"Q{dp}1-", h))
@@ -374,6 +371,28 @@
 
     gone = [give(k, sbuf.at[lax.rem(s + k, BLOCKS)], dbuf, a_send, a_recv) for k in ORDER]
     dbuf[pl.ds(s, 1)] = sbuf[pl.ds(s, 1)]
+    f_copy.wait()
+    high, low = halves(fs[...])
+    aspec[0:GROUP, :] = jnp.zeros((GROUP, FREQS), F32)
+    aspec[GROUP:, :] = dot(high, fbuf[0]) + dot(low, fbuf[0]) + dot(high, fbuf[1])
+    lane = lax.broadcasted_iota(jnp.int32, (GROUP, BLOCK), 1)
+    parity = 1.0 - 2.0 * lax.rem(lane, 2).astype(F32)
+
+    for table in (sre, sim, sre2):
+        table[BLOCK:, :] = jnp.zeros((LAG_PAD, BLOCK), F32)
+
+    def lag_piece(n, carry):
+        before = pl.ds(pl.multiple_of(n * GROUP, GROUP), GROUP)
+        after = pl.ds(pl.multiple_of(n * GROUP + GROUP, GROUP), GROUP)
+        re = aspec[before, 0:BLOCK] + parity * aspec[after, 0:BLOCK]
+        im = aspec[before, BLOCK:] + parity * aspec[after, BLOCK:]
+        sre[before, :] = re
+        sim[before, :] = jnp.where(lane == 0, 0.0, im)
+        sre2[before, :] = jnp.where(lane == 0, im, re)
+        return carry
+
+    lax.fori_loop(0, BLOCKS, lag_piece, 0)
+
     xs[0:LAG_PAD, :] = jnp.zeros((LAG_PAD, FREQS), F32)
     direct = skipcol[mine, :]
     direct = jnp.concatenate([direct, direct], axis=1)
@@ -433,64 +452,45 @@
     def half(h, dp, dq):
         return part.at[slot(h, dp, dq), pl.ds(h * 128, 128), :]
 
-    def straight(h, n):
-        dq, sign = ((2, 2), (1, 1), (3, -1))[n]
-        far_snd[h, n] = half(h, 2, dq)[...].astype(BF16)
-        sums.start(("F", h, n), far_snd.at[h, n], far_rcv.at[h, n], neighbour(h, 1, sign))
+    column = (2, 1, 3, 0)
 
     def relay(h, e):
-        snd[h, e, 0] = half(h, (1, 3, 0)[e], 2)[...].astype(BF16)
+        snd[h, e, 0] = half(h, column[e], 2)[...].astype(BF16)
         sums.start(("Q1+", h, e), snd.at[h, e, 0, pl.ds(0, 64), :], rq.at[h, e, 0], neighbour(h, 1, 1))
         sums.start(("Q1-", h, e), snd.at[h, e, 0, pl.ds(64, 64), :], rq.at[h, e, 1], neighbour(h, 1, -1))
 
-    for n in (1, 3):
-        project(n, 2)
-        relay(0, (n - 1) // 2)
-        project(2, n)
-        relay(1, (n - 1) // 2)
-    project(2, 2)
-    for h in (0, 1):
-        for n in (0, 1, 2):
-            straight(h, n)
-    project(0, 2)
-    relay(0, 2)
-    project(2, 0)
-    relay(1, 2)
+    for e in range(4):
+        for h in (0, 1):
+            if e or not h:
+                project(*((column[e], 2) if h == 0 else (2, column[e])))
+            relay(h, e)
     for dx, dy in ((1, 1), (1, 3), (3, 1), (3, 3), (0, 1), (1, 0), (0, 3), (3, 0), (0, 0)):
         project(dx, dy)
 
-    for e in (0, 1, 2):
-        dp = (1, 3, 0)[e]
+    for e in range(4):
         for h in (0, 1):
             sums.arrived(("Q1+", h, e))
-            one = half(h, dp, 1)
+            one = half(h, column[e], 1)
             snd[h, e, 1, 0:64] = (one[0:64, :] + rq[h, e, 0].astype(F32)).astype(BF16)
             snd[h, e, 1, 64:128] = one[64:128, :].astype(BF16)
             sums.start(("Q2+", h, e), snd.at[h, e, 1], rh.at[h, e, 0], neighbour(h, 1, 1))
             sums.arrived(("Q1-", h, e))
-            one = half(h, dp, 3)
+            one = half(h, column[e], 3)
             snd[h, e, 2, 0:64] = one[0:64, :].astype(BF16)
             snd[h, e, 2, 64:128] = (one[64:128, :] + rq[h, e, 1].astype(F32)).astype(BF16)
             sums.start(("Q2-", h, e), snd.at[h, e, 2], rh.at[h, e, 1], neighbour(h, 1, -1))
-    for h in (0, 1):
-        total = half(h, 2, 0)[...]
-        for n in (1, 2, 0):
-            sums.arrived(("F", h, n))
-            total = total + far_rcv[h, n].astype(F32)
-        psnd[h, 0] = total.astype(BF16)
-        sums.start(("P", h, 0), psnd.at[h, 0], rp.at[h, 0], neighbour(h, 0, 2))
 
     def reduced(h, e):
         sums.arrived(("Q2+", h, e))
         sums.arrived(("Q2-", h, e))
-        return half(h, (1, 3, 0)[e], 0)[...] + rh[h, e, 0].astype(F32) + rh[h, e, 1].astype(F32)
-
-    for e, sign in ((0, 1), (1, -1)):
+        return half(h, column[e], 0)[...] + rh[h, e, 0].astype(F32) + rh[h, e, 1].astype(F32)
+
+    for e, sign in ((0, 2), (1, 1), (2, -1)):
         for h in (0, 1):
-            psnd[h, 1 + e] = reduced(h, e).astype(BF16)
-            sums.start(("P", h, 1 + e), psnd.at[h, 1 + e], rp.at[h, 1 + e], neighbour(h, 0, sign))
-    for h in (0, 1):
-        red[h] = reduced(h, 2)
+            psnd[h, e] = reduced(h, e).astype(BF16)
+            sums.start(("P", h, e), psnd.at[h, e], rp.at[h, e], neighbour(h, 0, sign))
+    for h in (0, 1):
+        red[h] = reduced(h, 3)
     for h in (0, 1):
         total = red[h]
         for n in (0, 1, 2):
@@ -545,11 +545,9 @@
         pltpu.VMEM((BLOCKS, GROUP, BLOCK), BF16),
         pltpu.VMEM(square, BF16),
         pltpu.VMEM((16, *square), F32),
-        pltpu.VMEM((2, 3, 128, BLOCK), BF16),
-        pltpu.VMEM((2, 3, 128, BLOCK), BF16),
-        pltpu.VMEM((2, 3, 3, 128, BLOCK), BF16),
-        pltpu.VMEM((2, 3, 2, 64, BLOCK), BF16),
-        pltpu.VMEM((2, 3, 2, 128, BLOCK), BF16),
+        pltpu.VMEM((2, 4, 3, 128, BLOCK), BF16),
+        pltpu.VMEM((2, 4, 2, 64, BLOCK), BF16),
+        pltpu.VMEM((2, 4, 2, 128, BLOCK), BF16),
         pltpu.VMEM((2, 3, 128, BLOCK), BF16),
         pltpu.VMEM((2, 3, 128, BLOCK), BF16),
         pltpu.VMEM((2, 128, BLOCK), F32),
@@ -557,20 +555,20 @@
         dma((9,)),
         dma((16,)),
         dma((16,)),
-        dma((44,)),
-        dma((44,)),
+        dma((53,)),
+        dma((53,)),
         dma((1,)),
         dma((1,)),
         dma((16,)),
         dma((16,)),
         dma((16,)),
         dma((16,)),
-        dma((36,)),
-        dma((36,)),
+        dma((38,)),
+        dma((38,)),
     ]
     return pl.pallas_call(
         kernel,
-        out_shape=jax.ShapeDtypeStruct(square, BF16),
+        out_shape=pltpu.VMEM(square, BF16),
         in_specs=[hbm] * 11,
         out_specs=vmem,
         scratch_shapes=scratch,

time: 59.4 us -> 56.4 us (0.949)
  Pallas kernels: 57.7 us -> 55.6 us
  local copies, waits for them, and re-layouts: 1.57 us -> 0.66 us
    pallas_call x1, Pallas kernels: 57.7 us -> 55.6 us  [per_device(): pl.pallas_call(kernel, out_shape=pltpu.VMEM(square, BF16), in_specs=[hbm]...]
    unnamed x1, local copies, waits for them, and re-layouts: 1.57 us -> 0.66 us
where the time goes in v3:
time: 56.4 us; the launch traced here: 56.3 us
  Pallas kernels  55.6 us (99%)
  local copies, waits for them, and re-layouts  0.66 us (1%)
    pallas_call x1, Pallas kernels, per_device(): pl.pallas_call(kernel, out_shape=pltpu.VMEM(square, BF16), in_specs=[hbm]...  55.6 us

profile of v3, /device:TPU:1, one launch (start us, length us, event | category | flops | bytes accessed | tf_op | source)
XLA Modules:
  0.0 56.3 jit_solution(1792209321199064396)
XLA Ops:
  0.0 55.6 %hyena.1 = bf16[256,256]{1,0:T(8,128)(2,1)S(1)} custom-call(bf16[256,256]{1,0:T(8,128)(2,1)} %tok.1, bf16[3,4096,256]{2,1,0:T(8,128)(2,1)} %bitcast.3, f32[3,3,256]{2,1,0:T(4,128)} %taps_in.1, f32[33,64]{1,0:T(8,128)} %fin_in.1, f32[64,256]{1,0:T(8,128)} %fout_in.1, f32[1,256]{1,0:T(1,128)} %bitcast.4, f32[1,256]{1,0:T(1,128)} %bitcast.5, ...), custom_call_target="tpu_custom_call" | custom-call | tf_op jit(solution)/shard_map/hyena/pallas_call | solution.py:569
  55.6 0.7 %copy.13 = bf16[256,256]{1,0:T(8,128)(2,1)} copy(bf16[256,256]{1,0:T(8,128)(2,1)S(1)} %hyena.1) | data formatting | bytes 262144

commit v4 on v3

--- a/solution.py
+++ b/solution.py
@@ -325,6 +325,28 @@
         wo_copies[dx, dy] = pltpu.make_async_copy(wout.at[:, at], wo.at[n], wo_sem.at[n])
         wo_copies[dx, dy].start()
 
+    f_copy.wait()
+    high, low = halves(fs[...])
+    aspec[0:GROUP, :] = jnp.zeros((GROUP, FREQS), F32)
+    aspec[GROUP:, :] = dot(high, fbuf[0]) + dot(low, fbuf[0]) + dot(high, fbuf[1])
+    lane = lax.broadcasted_iota(jnp.int32, (GROUP, BLOCK), 1)
+    parity = 1.0 - 2.0 * lax.rem(lane, 2).astype(F32)
+
+    for table in (sre, sim, sre2):
+        table[BLOCK:, :] = jnp.zeros((LAG_PAD, BLOCK), F32)
+
+    def lag_piece(n, carry):
+        before = pl.ds(pl.multiple_of(n * GROUP, GROUP), GROUP)
+        after = pl.ds(pl.multiple_of(n * GROUP + GROUP, GROUP), GROUP)
+        re = aspec[before, 0:BLOCK] + parity * aspec[after, 0:BLOCK]
+        im = aspec[before, BLOCK:] + parity * aspec[after, BLOCK:]
+        sre[before, :] = re
+        sim[before, :] = jnp.where(lane == 0, 0.0, im)
+        sre2[before, :] = jnp.where(lane == 0, im, re)
+        return carry
+
+    lax.fori_loop(0, BLOCKS, lag_piece, 0)
+
     take("Q01+", "Q01-")
     multiply(order[1:11])
     for h, dp, block in ((0, 1, (1, 2)), (1, 1, (2, 1)), (0, 3, (3, 2)), (1, 3, (2, 3))):
@@ -356,55 +378,41 @@
 
     sbuf[...] = jnp.transpose(drv[...]).astype(BF16).reshape(BLOCKS, GROUP, BLOCK)
 
-    def give(k, src, dst, send, recv):
-        other = lax.rem(s + k, BLOCKS)
-        copy = pltpu.make_async_remote_copy(
+    def message(src, dst, send, recv, other):
+        return pltpu.make_async_remote_copy(
             src_ref=src,
             dst_ref=dst.at[s],
-            send_sem=send.at[k],
-            recv_sem=recv.at[k],
+            send_sem=send,
+            recv_sem=recv.at[s],
             device_id={"seq": other},
             device_id_type=MESH_ID,
         )
+
+    def got(j, buffer, send, recv):
+        @pl.when(s != j)
+        def _():
+            pltpu.make_async_remote_copy(
+                src_ref=buffer.at[j],
+                dst_ref=buffer.at[j],
+                send_sem=send.at[0],
+                recv_sem=recv.at[j],
+                device_id={"seq": lax.rem(s + 1, BLOCKS)},
+                device_id_type=MESH_ID,
+            ).wait_recv()
+
+    waits = [halo]
+    for k in ORDER:
+        other = lax.rem(s + k, BLOCKS)
+        copy = message(sbuf.at[other], dbuf, a_send.at[k], a_recv, other)
         copy.start()
-        return copy
-
-    gone = [give(k, sbuf.at[lax.rem(s + k, BLOCKS)], dbuf, a_send, a_recv) for k in ORDER]
+        waits.append(copy)
     dbuf[pl.ds(s, 1)] = sbuf[pl.ds(s, 1)]
-    f_copy.wait()
-    high, low = halves(fs[...])
-    aspec[0:GROUP, :] = jnp.zeros((GROUP, FREQS), F32)
-    aspec[GROUP:, :] = dot(high, fbuf[0]) + dot(low, fbuf[0]) + dot(high, fbuf[1])
-    lane = lax.broadcasted_iota(jnp.int32, (GROUP, BLOCK), 1)
-    parity = 1.0 - 2.0 * lax.rem(lane, 2).astype(F32)
-
-    for table in (sre, sim, sre2):
-        table[BLOCK:, :] = jnp.zeros((LAG_PAD, BLOCK), F32)
-
-    def lag_piece(n, carry):
-        before = pl.ds(pl.multiple_of(n * GROUP, GROUP), GROUP)
-        after = pl.ds(pl.multiple_of(n * GROUP + GROUP, GROUP), GROUP)
-        re = aspec[before, 0:BLOCK] + parity * aspec[after, 0:BLOCK]
-        im = aspec[before, BLOCK:] + parity * aspec[after, BLOCK:]
-        sre[before, :] = re
-        sim[before, :] = jnp.where(lane == 0, 0.0, im)
-        sre2[before, :] = jnp.where(lane == 0, im, re)
-        return carry
-
-    lax.fori_loop(0, BLOCKS, lag_piece, 0)
-
     xs[0:LAG_PAD, :] = jnp.zeros((LAG_PAD, FREQS), F32)
     direct = skipcol[mine, :]
     direct = jnp.concatenate([direct, direct], axis=1)
     g_copy.wait()
-    for copy in gone:
-        copy.wait_recv()
-    waits = [halo] + gone
-
-    drive = dbuf[...].reshape(BLOCK, BLOCK)
-    xs[LAG_PAD:, :] = dot(drive, fbuf[0]) + dot(drive, fbuf[1])
-
-    def spectrum(n, i):
+
+    def spectrum(i):
         def lags(turn, total):
             re, im = total
             for d in range(LAG_STEP):
@@ -418,27 +426,32 @@
             return re, im
 
         zero = jnp.zeros((GROUP, BLOCK), F32)
-        re, im = lax.fori_loop(0, lax.div(i + LAG_STEP, LAG_STEP), lags, (zero, zero))
-        ys[n * GROUP : (n + 1) * GROUP, 0:BLOCK] = re
-        ys[n * GROUP : (n + 1) * GROUP, BLOCK:] = im
-
-    steps = ORDER + (0,)
-    for start in (0, 8):
-        for n in range(start, start + 8):
-            spectrum(n, lax.rem(s + steps[n], BLOCKS))
-        some = slice(start * GROUP, start * GROUP + 8 * GROUP)
+        re, im = lax.fori_loop(0, (i + LAG_STEP) // LAG_STEP, lags, (zero, zero))
+        ys[i * GROUP : (i + 1) * GROUP, 0:BLOCK] = re
+        ys[i * GROUP : (i + 1) * GROUP, BLOCK:] = im
+
+    returns = []
+    for low_block, high_block in ((0, 4), (4, 8), (8, 16)):
+        count = (high_block - low_block) * GROUP
+        for j in range(low_block, high_block):
+            got(j, dbuf, a_send, a_recv)
+        some = slice(low_block * GROUP, high_block * GROUP)
+        drive = dbuf[low_block:high_block].reshape(count, BLOCK)
+        xs[LAG_PAD + some.start : LAG_PAD + some.stop, :] = dot(drive, fbuf[0]) + dot(drive, fbuf[1])
+        for i in range(low_block, high_block):
+            spectrum(i)
         high, low = halves(ys[some, :])
         both = dot(jnp.concatenate([high, low], axis=0), gbuf[0])
-        conv = both[: 8 * GROUP] + both[8 * GROUP :] + dot(high, gbuf[1])
-        for n in range(start, start + 8):
-            i = lax.rem(s + steps[n], BLOCKS)
-            value = conv[(n - start) * GROUP : (n - start + 1) * GROUP, :]
-            cbuf[n] = (value + direct * dbuf[i].astype(F32)).astype(BF16)
-            if steps[n]:
-                waits.append(give(steps[n], cbuf.at[n], rbuf, b_send, b_recv))
-    rbuf[pl.ds(s, 1)] = cbuf[pl.ds(BLOCKS - 1, 1)]
-    for copy in waits[-15:]:
-        copy.wait_recv()
+        conv = both[:count] + both[count:] + dot(high, gbuf[1])
+        for i in range(low_block, high_block):
+            value = conv[(i - low_block) * GROUP : (i - low_block + 1) * GROUP, :]
+            cbuf[i] = (value + direct * dbuf[i].astype(F32)).astype(BF16)
+            copy = message(cbuf.at[i], rbuf, b_send.at[i], b_recv, i)
+            returns.append(copy)
+            pl.when(s != i)(copy.start)
+    rbuf[pl.ds(s, 1)] = cbuf[pl.ds(s, 1)]
+    for j in range(BLOCKS):
+        got(j, rbuf, b_send, b_recv)
 
     back = jnp.transpose(rbuf[...].reshape(BLOCK, BLOCK).astype(F32))
     gated[...] = (qbuf[...] * back).astype(BF16)
@@ -464,25 +477,42 @@
             if e or not h:
                 project(*((column[e], 2) if h == 0 else (2, column[e])))
             relay(h, e)
-    for dx, dy in ((1, 1), (1, 3), (3, 1), (3, 3), (0, 1), (1, 0), (0, 3), (3, 0), (0, 0)):
-        project(dx, dy)
-
-    for e in range(4):
+    def pass_on(name, h, e, n, start, value):
+        there = pl.ds(start, 64)
+        snd[h, e, n, there, :] = value.astype(BF16)
+        sums.start(
+            (name, h, e, n), snd.at[h, e, n, there, :], rh.at[h, e, n - 1, there, :], neighbour(h, 1, 3 - 2 * n)
+        )
+
+    def free(e):
+        for h in (0, 1):
+            pass_on("free", h, e, 1, 64, half(h, column[e], 1)[64:128, :])
+            pass_on("free", h, e, 2, 0, half(h, column[e], 3)[0:64, :])
+
+    def joined(e):
         for h in (0, 1):
             sums.arrived(("Q1+", h, e))
-            one = half(h, column[e], 1)
-            snd[h, e, 1, 0:64] = (one[0:64, :] + rq[h, e, 0].astype(F32)).astype(BF16)
-            snd[h, e, 1, 64:128] = one[64:128, :].astype(BF16)
-            sums.start(("Q2+", h, e), snd.at[h, e, 1], rh.at[h, e, 0], neighbour(h, 1, 1))
+            pass_on("joined", h, e, 1, 0, half(h, column[e], 1)[0:64, :] + rq[h, e, 0].astype(F32))
             sums.arrived(("Q1-", h, e))
-            one = half(h, column[e], 3)
-            snd[h, e, 2, 0:64] = one[0:64, :].astype(BF16)
-            snd[h, e, 2, 64:128] = (one[64:128, :] + rq[h, e, 1].astype(F32)).astype(BF16)
-            sums.start(("Q2-", h, e), snd.at[h, e, 2], rh.at[h, e, 1], neighbour(h, 1, -1))
+            pass_on("joined", h, e, 2, 64, half(h, column[e], 3)[64:128, :] + rq[h, e, 1].astype(F32))
+
+    free(0)
+    for dx, dy in ((1, 1), (1, 3), (3, 1)):
+        project(dx, dy)
+    free(1)
+    project(3, 3)
+    free(2)
+    for dx, dy in ((0, 1), (1, 0), (0, 3), (3, 0), (0, 0)):
+        project(dx, dy)
+    for e in (0, 1, 2):
+        joined(e)
+    free(3)
+    joined(3)
 
     def reduced(h, e):
-        sums.arrived(("Q2+", h, e))
-        sums.arrived(("Q2-", h, e))
+        for name in ("free", "joined"):
+            for n in (1, 2):
+                sums.arrived((name, h, e, n))
         return half(h, column[e], 0)[...] + rh[h, e, 0].astype(F32) + rh[h, e, 1].astype(F32)
 
     for e, sign in ((0, 2), (1, 1), (2, -1)):
@@ -502,6 +532,8 @@
     sums.finish()
     for copy in waits:
         copy.wait_send()
+    for i, copy in enumerate(returns):
+        pl.when(s != i)(copy.wait_send)
 
 
 def per_device(tokens, in_weight, short_taps, filter_in, filter_out, rates, skip, out_weight):
@@ -563,8 +595,8 @@
         dma((16,)),
         dma((16,)),
         dma((16,)),
-        dma((38,)),
-        dma((38,)),
+        dma((54,)),
+        dma((54,)),
     ]
     return pl.pallas_call(
         kernel,

time: 56.4 us -> 55 us (0.975)
  Pallas kernels: 55.6 us -> 54.3 us
    pallas_call x1, Pallas kernels: 55.6 us -> 54.3 us  [per_device(): pl.pallas_call(kernel, out_shape=pltpu.VMEM(square, BF16), in_specs=[hbm]...]
where the time goes in v4:
time: 55 us
  Pallas kernels  54.3 us (99%)
  local copies, waits for them, and re-layouts  0.66 us (1%)
    pallas_call x1, Pallas kernels, per_device(): pl.pallas_call(kernel, out_shape=pltpu.VMEM(square, BF16), in_specs=[hbm]...  54.3 us

profile of v4, /device:TPU:1, one launch (start us, length us, event | category | flops | bytes accessed | tf_op | source)
XLA Modules:
  0.0 55.0 jit_solution(12739172246430320047)
XLA Ops:
  0.0 54.3 %hyena.1 = bf16[256,256]{1,0:T(8,128)(2,1)S(1)} custom-call(bf16[256,256]{1,0:T(8,128)(2,1)} %tok.1, bf16[3,4096,256]{2,1,0:T(8,128)(2,1)} %bitcast.3, f32[3,3,256]{2,1,0:T(4,128)} %taps_in.1, f32[33,64]{1,0:T(8,128)} %fin_in.1, f32[64,256]{1,0:T(8,128)} %fout_in.1, f32[1,256]{1,0:T(1,128)} %bitcast.4, f32[1,256]{1,0:T(1,128)} %bitcast.5, ...), custom_call_target="tpu_custom_call" | custom-call | tf_op jit(solution)/shard_map/hyena/pallas_call | solution.py:601
  54.3 0.7 %copy.13 = bf16[256,256]{1,0:T(8,128)(2,1)} copy(bf16[256,256]{1,0:T(8,128)(2,1)S(1)} %hyena.1) | data formatting | bytes 262144

commit v5 on v4

--- a/solution.py
+++ b/solution.py
@@ -325,28 +325,6 @@
         wo_copies[dx, dy] = pltpu.make_async_copy(wout.at[:, at], wo.at[n], wo_sem.at[n])
         wo_copies[dx, dy].start()
 
-    f_copy.wait()
-    high, low = halves(fs[...])
-    aspec[0:GROUP, :] = jnp.zeros((GROUP, FREQS), F32)
-    aspec[GROUP:, :] = dot(high, fbuf[0]) + dot(low, fbuf[0]) + dot(high, fbuf[1])
-    lane = lax.broadcasted_iota(jnp.int32, (GROUP, BLOCK), 1)
-    parity = 1.0 - 2.0 * lax.rem(lane, 2).astype(F32)
-
-    for table in (sre, sim, sre2):
-        table[BLOCK:, :] = jnp.zeros((LAG_PAD, BLOCK), F32)
-
-    def lag_piece(n, carry):
-        before = pl.ds(pl.multiple_of(n * GROUP, GROUP), GROUP)
-        after = pl.ds(pl.multiple_of(n * GROUP + GROUP, GROUP), GROUP)
-        re = aspec[before, 0:BLOCK] + parity * aspec[after, 0:BLOCK]
-        im = aspec[before, BLOCK:] + parity * aspec[after, BLOCK:]
-        sre[before, :] = re
-        sim[before, :] = jnp.where(lane == 0, 0.0, im)
-        sre2[before, :] = jnp.where(lane == 0, im, re)
-        return carry
-
-    lax.fori_loop(0, BLOCKS, lag_piece, 0)
-
     take("Q01+", "Q01-")
     multiply(order[1:11])
     for h, dp, block in ((0, 1, (1, 2)), (1, 1, (2, 1)), (0, 3, (3, 2)), (1, 3, (2, 3))):
@@ -407,6 +385,28 @@
         copy.start()
         waits.append(copy)
     dbuf[pl.ds(s, 1)] = sbuf[pl.ds(s, 1)]
+    f_copy.wait()
+    high, low = halves(fs[...])
+    aspec[0:GROUP, :] = jnp.zeros((GROUP, FREQS), F32)
+    aspec[GROUP:, :] = dot(high, fbuf[0]) + dot(low, fbuf[0]) + dot(high, fbuf[1])
+    lane = lax.broadcasted_iota(jnp.int32, (GROUP, BLOCK), 1)
+    parity = 1.0 - 2.0 * lax.rem(lane, 2).astype(F32)
+
+    for table in (sre, sim, sre2):
+        table[BLOCK:, :] = jnp.zeros((LAG_PAD, BLOCK), F32)
+
+    def lag_piece(n, carry):
+        before = pl.ds(pl.multiple_of(n * GROUP, GROUP), GROUP)
+        after = pl.ds(pl.multiple_of(n * GROUP + GROUP, GROUP), GROUP)
+        re = aspec[before, 0:BLOCK] + parity * aspec[after, 0:BLOCK]
+        im = aspec[before, BLOCK:] + parity * aspec[after, BLOCK:]
+        sre[before, :] = re
+        sim[before, :] = jnp.where(lane == 0, 0.0, im)
+        sre2[before, :] = jnp.where(lane == 0, im, re)
+        return carry
+
+    lax.fori_loop(0, BLOCKS, lag_piece, 0)
+
     xs[0:LAG_PAD, :] = jnp.zeros((LAG_PAD, FREQS), F32)
     direct = skipcol[mine, :]
     direct = jnp.concatenate([direct, direct], axis=1)

time: 55 us -> 54.4 us (0.989)
  Pallas kernels: 54.3 us -> 53.7 us
    pallas_call x1, Pallas kernels: 54.3 us -> 53.7 us  [per_device(): pl.pallas_call(kernel, out_shape=pltpu.VMEM(square, BF16), in_specs=[hbm]...]
where the time goes in v5:
time: 54.4 us; the launch traced here: 54.3 us
  Pallas kernels  53.7 us (99%)
  local copies, waits for them, and re-layouts  0.66 us (1%)
    pallas_call x1, Pallas kernels, per_device(): pl.pallas_call(kernel, out_shape=pltpu.VMEM(square, BF16), in_specs=[hbm]...  53.7 us

profile of v5, /device:TPU:1, one launch (start us, length us, event | category | flops | bytes accessed | tf_op | source)
XLA Modules:
  0.0 54.3 jit_solution(13317671263530084144)
XLA Ops:
  0.0 53.7 %hyena.1 = bf16[256,256]{1,0:T(8,128)(2,1)S(1)} custom-call(bf16[256,256]{1,0:T(8,128)(2,1)} %tok.1, bf16[3,4096,256]{2,1,0:T(8,128)(2,1)} %bitcast.3, f32[3,3,256]{2,1,0:T(4,128)} %taps_in.1, f32[33,64]{1,0:T(8,128)} %fin_in.1, f32[64,256]{1,0:T(8,128)} %fout_in.1, f32[1,256]{1,0:T(1,128)} %bitcast.4, f32[1,256]{1,0:T(1,128)} %bitcast.5, ...), custom_call_target="tpu_custom_call" | custom-call | tf_op jit(solution)/shard_map/hyena/pallas_call | solution.py:601
  53.7 0.7 %copy.13 = bf16[256,256]{1,0:T(8,128)(2,1)} copy(bf16[256,256]{1,0:T(8,128)(2,1)S(1)} %hyena.1) | data formatting | bytes 262144

commit v6 on v5

--- a/solution.py
+++ b/solution.py
@@ -144,9 +144,21 @@
     barrier = pltpu.get_barrier_semaphore()
     near = [{"chan": chan_at(step, 0)} for step in (1, -1, 2)]
     near += [{"chan": chan_at(0, step)} for step in (1, -1, 2)]
-    near += [sibling, plane(1), plane(-1)]
+    near += [sibling]
     for device in near:
         pl.semaphore_signal(barrier, inc=1, device_id=device, device_id_type=MESH_ID)
+
+    def planes(step):
+        return (z < 8 - step).astype(jnp.int32) + (z >= step).astype(jnp.int32)
+
+    def greet(semaphore, step):
+        for there, sign in ((z < 8 - step, step), (z >= step, -step)):
+
+            @pl.when(there)
+            def _():
+                pl.semaphore_signal(semaphore, inc=1, device_id=plane(sign), device_id_type=MESH_ID)
+
+    greet(barrier, 1)
 
     small = [
         pltpu.make_async_copy(src, dst, local_sem.at[4 + n])
@@ -176,16 +188,16 @@
     start_weights(0, 1)
     wo_copies = {}
 
-    pl.semaphore_wait(barrier, len(near))
-
-    rounds = ([plane(1), plane(-1)], [plane(2), plane(-2)], [sibling])
+    pl.semaphore_wait(barrier, len(near) + planes(1))
 
     def tell(n):
-        for device in rounds[n]:
-            pl.semaphore_signal(word_sem.at[n], inc=1, device_id=device, device_id_type=MESH_ID)
+        if n == 3:
+            pl.semaphore_signal(word_sem.at[n], inc=1, device_id=sibling, device_id_type=MESH_ID)
+        else:
+            greet(word_sem.at[n], 1 << n)
 
     def hear(n):
-        pl.semaphore_wait(word_sem.at[n], len(rounds[n]))
+        pl.semaphore_wait(word_sem.at[n], 1 if n == 3 else planes(1 << n))
 
     links = Links(ag_send, ag_recv)
 
@@ -297,6 +309,9 @@
         push("Q21+", h, (2, 1), (2, 2), "q1", 1, 1)
         push("Q21-", h, (2, 3), (2, 2), "q2", 1, -1)
 
+    hear(1)
+    tell(2)
+
     for step in (1, 2, 3):
         for k in range(4):
             links.arrived(("EQ", step, k))
@@ -316,9 +331,7 @@
         device_id={"seq": lax.rem(s + 1, BLOCKS)},
         device_id_type=MESH_ID,
     )
-    halo.start()
-    hear(1)
-    tell(2)
+    pl.when(s < BLOCKS - 1)(halo.start)
     g_copy.start()
     for n, (dx, dy) in enumerate(spots):
         at = pl.ds(pl.multiple_of(chan_at(dx, dy) * BLOCK, BLOCK), BLOCK)
@@ -327,11 +340,12 @@
 
     take("Q01+", "Q01-")
     multiply(order[1:11])
+    hear(2)
+    tell(3)
     for h, dp, block in ((0, 1, (1, 2)), (1, 1, (2, 1)), (0, 3, (3, 2)), (1, 3, (2, 3))):
         links.arrived((f"Q{dp}1+", h))
         links.arrived((f"Q{dp}1-", h))
         multiply([block])
-    hear(2)
     take("Q21+", "Q21-")
     multiply([(2, 2)])
 
@@ -347,10 +361,14 @@
         qbuf[pl.ds(start, size), :] = branch[0]
         drv[pl.ds(start, size), :] = branch[1] * branch[2]
 
-    halo.wait_recv()
-    live = (s > 0).astype(F32)
+    pl.when(s > 0)(halo.wait_recv)
+
+    @pl.when(s == 0)
+    def _():
+        edge_in[...] = jnp.zeros_like(edge_in)
+
     for j in range(3):
-        pf[j, 0:16, :] = edge_in[j].astype(F32) * live
+        pf[j, 0:16, :] = edge_in[j].astype(F32)
     for start in range(0, BLOCK, 32):
         short(start, 32)
 
@@ -378,7 +396,8 @@
                 device_id_type=MESH_ID,
             ).wait_recv()
 
-    waits = [halo]
+    hear(3)
+    waits = []
     for k in ORDER:
         other = lax.rem(s + k, BLOCKS)
         copy = message(sbuf.at[other], dbuf, a_send.at[k], a_recv, other)
@@ -386,9 +405,7 @@
         waits.append(copy)
     dbuf[pl.ds(s, 1)] = sbuf[pl.ds(s, 1)]
     f_copy.wait()
-    high, low = halves(fs[...])
     aspec[0:GROUP, :] = jnp.zeros((GROUP, FREQS), F32)
-    aspec[GROUP:, :] = dot(high, fbuf[0]) + dot(low, fbuf[0]) + dot(high, fbuf[1])
     lane = lax.broadcasted_iota(jnp.int32, (GROUP, BLOCK), 1)
     parity = 1.0 - 2.0 * lax.rem(lane, 2).astype(F32)
 
@@ -405,7 +422,13 @@
         sre2[before, :] = jnp.where(lane == 0, im, re)
         return carry
 
-    lax.fori_loop(0, BLOCKS, lag_piece, 0)
+    def lag_spectra(first, last):
+        high, low = halves(fs[first * GROUP : last * GROUP, :])
+        spectra = dot(high, fbuf[0]) + dot(low, fbuf[0]) + dot(high, fbuf[1])
+        aspec[(first + 1) * GROUP : (last + 1) * GROUP, :] = spectra
+        lax.fori_loop(first, last, lag_piece, 0)
+
+    lag_spectra(0, 4)
 
     xs[0:LAG_PAD, :] = jnp.zeros((LAG_PAD, FREQS), F32)
     direct = skipcol[mine, :]
@@ -449,6 +472,8 @@
             copy = message(cbuf.at[i], rbuf, b_send.at[i], b_recv, i)
             returns.append(copy)
             pl.when(s != i)(copy.start)
+        if low_block == 0:
+            lag_spectra(4, BLOCKS)
     rbuf[pl.ds(s, 1)] = cbuf[pl.ds(s, 1)]
     for j in range(BLOCKS):
         got(j, rbuf, b_send, b_recv)
@@ -532,6 +557,7 @@
     sums.finish()
     for copy in waits:
         copy.wait_send()
+    pl.when(s < BLOCKS - 1)(halo.wait_send)
     for i, copy in enumerate(returns):
         pl.when(s != i)(copy.wait_send)
 
@@ -583,7 +609,7 @@
         pltpu.VMEM((2, 3, 128, BLOCK), BF16),
         pltpu.VMEM((2, 3, 128, BLOCK), BF16),
         pltpu.VMEM((2, 128, BLOCK), F32),
-        pltpu.SemaphoreType.REGULAR((3,)),
+        pltpu.SemaphoreType.REGULAR((4,)),
         dma((9,)),
         dma((16,)),
         dma((16,)),

time: 54.4 us -> 54.1 us (level)
  no operation moved by 1% of the time
where the time goes in v6:
time: 54.1 us; the launch traced here: 54 us
  Pallas kernels  53.3 us (99%)
  local copies, waits for them, and re-layouts  0.66 us (1%)
    pallas_call x1, Pallas kernels, per_device(): pl.pallas_call(kernel, out_shape=pltpu.VMEM(square, BF16), in_specs=[hbm]...  53.3 us

profile of v6, /device:TPU:1, one launch (start us, length us, event | category | flops | bytes accessed | tf_op | source)
XLA Modules:
  0.0 54.0 jit_solution(426962822099851790)
XLA Ops:
  0.0 53.3 %hyena.1 = bf16[256,256]{1,0:T(8,128)(2,1)S(1)} custom-call(bf16[256,256]{1,0:T(8,128)(2,1)} %tok.1, bf16[3,4096,256]{2,1,0:T(8,128)(2,1)} %bitcast.3, f32[3,3,256]{2,1,0:T(4,128)} %taps_in.1, f32[33,64]{1,0:T(8,128)} %fin_in.1, f32[64,256]{1,0:T(8,128)} %fout_in.1, f32[1,256]{1,0:T(1,128)} %bitcast.4, f32[1,256]{1,0:T(1,128)} %bitcast.5, ...), custom_call_target="tpu_custom_call" | custom-call | tf_op jit(solution)/shard_map/hyena/pallas_call | solution.py:627
  53.3 0.7 %copy.13 = bf16[256,256]{1,0:T(8,128)(2,1)} copy(bf16[256,256]{1,0:T(8,128)(2,1)S(1)} %hyena.1) | data formatting | bytes 262144

commit v7 on v6

--- a/solution.py
+++ b/solution.py
@@ -546,13 +546,6 @@
             sums.start(("P", h, e), psnd.at[h, e], rp.at[h, e], neighbour(h, 0, sign))
     for h in (0, 1):
         red[h] = reduced(h, 3)
-    for h in (0, 1):
-        total = red[h]
-        for n in (0, 1, 2):
-            sums.arrived(("P", h, n))
-            total = total + rp[h, n].astype(F32)
-        out[h * 128 : h * 128 + 128, :] = total.astype(BF16)
-
     links.finish()
     sums.finish()
     for copy in waits:
@@ -560,6 +553,12 @@
     pl.when(s < BLOCKS - 1)(halo.wait_send)
     for i, copy in enumerate(returns):
         pl.when(s != i)(copy.wait_send)
+    for h in (0, 1):
+        total = red[h]
+        for n in (0, 1, 2):
+            sums.arrived(("P", h, n))
+            total = total + rp[h, n].astype(F32)
+        out[h * 128 : h * 128 + 128, :] = total.astype(BF16)
 
 
 def per_device(tokens, in_weight, short_taps, filter_in, filter_out, rates, skip, out_weight):

time: 54.1 us -> 53.8 us (level)
  no operation moved by 1% of the time
where the time goes in v7:
time: 53.8 us
  Pallas kernels  53.1 us (99%)
  local copies, waits for them, and re-layouts  0.66 us (1%)
    pallas_call x1, Pallas kernels, per_device(): pl.pallas_call(kernel, out_shape=pltpu.VMEM(square, BF16), in_specs=[hbm]...  53.1 us

profile of v7, /device:TPU:1, one launch (start us, length us, event | category | flops | bytes accessed | tf_op | source)
XLA Modules:
  0.0 53.8 jit_solution(435659320193972273)
XLA Ops:
  0.0 53.1 %hyena.1 = bf16[256,256]{1,0:T(8,128)(2,1)S(1)} custom-call(bf16[256,256]{1,0:T(8,128)(2,1)} %tok.1, bf16[3,4096,256]{2,1,0:T(8,128)(2,1)} %bitcast.3, f32[3,3,256]{2,1,0:T(4,128)} %taps_in.1, f32[33,64]{1,0:T(8,128)} %fin_in.1, f32[64,256]{1,0:T(8,128)} %fout_in.1, f32[1,256]{1,0:T(1,128)} %bitcast.4, f32[1,256]{1,0:T(1,128)} %bitcast.5, ...), custom_call_target="tpu_custom_call" | custom-call | tf_op jit(solution)/shard_map/hyena/pallas_call | solution.py:626
  53.1 0.7 %copy.13 = bf16[256,256]{1,0:T(8,128)(2,1)} copy(bf16[256,256]{1,0:T(8,128)(2,1)S(1)} %hyena.1) | data formatting | bytes 262144
